TPU v7x, 32 devices: a whole 2x2x4 slice. The times are simulated.
32 devices in a mesh: groups: 2 (over y), expert: 4 (over x, core), seq: 4 (over z).
Axes of the slice: x: 2, y: 2, z: 4, core: 2. Of those that a mesh axis runs over, the one named last changes fastest.
Arguments:
- tokens: bfloat16 [1024, 7168], P(('groups', 'seq'), 'expert'), parts along dimension 0, may hold values from -6 to 6
- out_grad: bfloat16 [1024, 7168], P(('groups', 'seq'), 'expert'), parts along dimension 0, may hold values from -3 to 3
- routes: int32 [1024, 8], P('groups'), parts along dimension 0, may hold values from 0 to 15, all different within a row; in each aligned block of 128 rows (0 to 127, 128 to 255, ...) at most 80 rows name the same one
- route_weights: float32 [1024, 8], P('groups'), parts along dimension 0, may hold values from 0.05 to 0.5
- w_gate: bfloat16 [16, 7168, 1024], P('expert', None, 'seq'), may hold values from -0.0625 to 0.0625
- w_up: bfloat16 [16, 7168, 1024], P('expert', None, 'seq'), may hold values from -0.0625 to 0.0625
- w_down: bfloat16 [16, 1024, 7168], P('expert', 'seq'), may hold values from -0.1875 to 0.1875
Outputs:
- token_grad: bfloat16 [1024, 7168], P(('groups', 'seq'), 'expert'), parts along dimension 0
- weight_grad_gate: bfloat16 [32, 7168, 1024], P(('groups', 'expert'), None, 'seq'), parts along dimension 0
- weight_grad_up: bfloat16 [32, 7168, 1024], P(('groups', 'expert'), None, 'seq'), parts along dimension 0
- weight_grad_down: bfloat16 [32, 1024, 7168], P(('groups', 'expert'), 'seq'), parts along dimension 0
- gate_grad: float32 [1024, 8], P(('groups', 'seq')), parts along dimension 0
There are 2 independent parts, one for each index of `groups`. A program takes and returns all parts, laid end to end along the dimension named above; an argument that names none is the same for every part. Nothing has to cross between parts.
Inputs may be any that keep to these rules, and one draw needn't show every extreme that they name: `routes`: each row names 8 different experts. In each aligned block of 128 rows no expert is named by more than 80 rows, a bound that some block reaches.
All inputs are finite; a program needn't handle non-finite values.
Results may differ from a plain program's by a relative error of at most 0.012.
Values may be sent and summed in bfloat16 or wider, within the bound.
A program may use at most 384 MiB of HBM per device.

v0:
```python
import jax
import jax.numpy as jnp
from jax import lax
from jax.sharding import PartitionSpec as P

CAP = 80


def body(tokens, out_grad, routes, route_weights, w_gate, w_up, w_down):
    shards = lax.axis_size("seq")
    seq_owner = lax.axis_index("seq")
    tok_rows, features = tokens.shape
    top_count = routes.shape[1]
    local_experts = w_gate.shape[0]
    block_width = w_gate.shape[2]
    experts = local_experts * lax.axis_size("expert")
    capacity = CAP
    slot_rows = shards * capacity
    first_expert = lax.axis_index("expert") * local_experts
    shard_routes = routes.reshape(shards, tok_rows, top_count)
    shard_weights = route_weights.reshape(shards, tok_rows, top_count)
    expert_ids = jnp.arange(experts, dtype=jnp.int32)
    hit_table = (shard_routes[:, :, :, None] == expert_ids[None, None, None, :]).astype(jnp.int32)
    member_of = jnp.sum(hit_table, axis=2)
    ranked = jnp.cumsum(member_of, axis=1) - member_of
    slot_of = jnp.sum(hit_table * ranked[:, :, None, :], axis=3)
    shard_ids = jnp.broadcast_to(
        jnp.arange(shards, dtype=jnp.int32)[:, None, None], shard_routes.shape
    )
    row_ids = jnp.broadcast_to(
        jnp.arange(tok_rows, dtype=jnp.int32)[None, :, None], shard_routes.shape
    )
    source = (
        jnp.full((shards, experts, capacity), tok_rows, jnp.int32)
        .at[shard_ids, shard_routes, slot_of]
        .set(row_ids)
    )
    weights_all = (
        jnp.zeros((experts, slot_rows), jnp.float32)
        .at[shard_routes, shard_ids * capacity + slot_of]
        .set(shard_weights)
    )
    row_weight = lax.dynamic_slice_in_dim(weights_all, first_expert, local_experts, 0)
    zero_row = jnp.zeros((1, features), tokens.dtype)
    own_source = lax.dynamic_index_in_dim(source, seq_owner, 0, keepdims=False)
    send_tokens = jnp.concatenate([tokens, zero_row], 0)[own_source]
    send_grads = jnp.concatenate([out_grad, zero_row], 0)[own_source]
    local_tokens, local_grads = (
        lax.all_to_all(send_tokens, "expert", split_axis=0, concat_axis=2, tiled=True),
        lax.all_to_all(send_grads, "expert", split_axis=0, concat_axis=2, tiled=True),
    )
    rows_in, grads_in = (
        lax.all_gather(local_tokens, "seq", axis=1, tiled=True),
        lax.all_gather(local_grads, "seq", axis=1, tiled=True),
    )
    joined_weights = jnp.concatenate([w_gate, w_up], axis=2)
    pre_both = jnp.einsum(
        "ezd,edh->ezh", rows_in, joined_weights, preferred_element_type=jnp.float32
    )
    pre_gate = pre_both[:, :, :block_width]
    pre_up = pre_both[:, :, block_width:]
    sigmoid_gate = jax.nn.sigmoid(pre_gate)
    activated = pre_gate * sigmoid_gate * pre_up
    back_grad = jnp.einsum("ezd,ehd->ezh", grads_in, w_down, preferred_element_type=jnp.float32)
    scores = jnp.sum(activated * back_grad, axis=2)
    scaled = row_weight[:, :, None] * back_grad
    up_grad = (scaled * pre_gate * sigmoid_gate).astype(jnp.bfloat16)
    pre_grad = (scaled * pre_up * sigmoid_gate * (1.0 + pre_gate * (1.0 - sigmoid_gate))).astype(
        jnp.bfloat16
    )
    scaled_act = (row_weight[:, :, None] * activated).astype(jnp.bfloat16)
    joined_grads = jnp.concatenate([pre_grad, up_grad], axis=2)
    grad_down = jnp.einsum(
        "ezh,ezd->ehd", scaled_act, grads_in, preferred_element_type=jnp.float32
    ).astype(jnp.bfloat16)
    grad_both = jnp.einsum(
        "ezd,ezh->edh", rows_in, joined_grads, preferred_element_type=jnp.float32
    ).astype(jnp.bfloat16)
    grad_gate = grad_both[:, :, :block_width]
    grad_up = grad_both[:, :, block_width:]
    row_grads = jnp.einsum(
        "ezh,edh->ezd", joined_grads, joined_weights, preferred_element_type=jnp.float32
    )
    own_routes = lax.dynamic_slice_in_dim(routes, seq_owner * tok_rows, tok_rows, 0)
    own_slots = lax.dynamic_index_in_dim(slot_of, seq_owner, 0, keepdims=False)
    arrived = lax.all_to_all(
        row_grads.astype(jnp.bfloat16), "expert", split_axis=2, concat_axis=0, tiled=True
    )
    segment_start = (jnp.arange(shards, dtype=jnp.int32) * capacity)[:, None, None]
    row_index = (shard_routes * slot_rows + segment_start + slot_of).reshape(
        shards * tok_rows, top_count
    )
    flat_rows = arrived.reshape(experts * slot_rows, features)
    token_sum = jnp.zeros((shards * tok_rows, features), jnp.float32)
    for column in range(top_count):
        token_sum = token_sum + flat_rows[row_index[:, column]].astype(jnp.float32)
    score_blocks = jnp.transpose(scores.reshape(local_experts, shards, capacity), (1, 0, 2))
    token_part, score_part = (
        lax.psum_scatter(
            token_sum.astype(jnp.bfloat16), "seq", scatter_dimension=0, tiled=True
        ).astype(jnp.float32),
        lax.psum_scatter(
            score_blocks.astype(jnp.bfloat16), "seq", scatter_dimension=0, tiled=True
        ).astype(jnp.float32),
    )
    token_grad = token_part.astype(jnp.bfloat16)
    own_scores = score_part[0]
    local_ids = first_expert + jnp.arange(local_experts, dtype=jnp.int32)
    is_local = own_routes[:, :, None] == local_ids[None, None, :]
    expert_slots = jnp.arange(local_experts, dtype=jnp.int32)[None, None, :]
    picked = own_scores[expert_slots, own_slots[:, :, None]]
    gate_part = jnp.sum(jnp.where(is_local, picked, 0.0), axis=2)
    gate_grad = lax.psum(gate_part, "expert")
    return (token_grad, grad_gate, grad_up, grad_down, gate_grad)


def solution(mesh):
    in_specs = (
        P(("groups", "seq"), "expert"),
        P(("groups", "seq"), "expert"),
        P("groups", None),
        P("groups", None),
        P("expert", None, "seq"),
        P("expert", None, "seq"),
        P("expert", "seq", None),
    )
    out_specs = (
        P(("groups", "seq"), "expert"),
        P(("groups", "expert"), None, "seq"),
        P(("groups", "expert"), None, "seq"),
        P(("groups", "expert"), "seq", None),
        P(("groups", "seq"), None),
    )
    return jax.shard_map(body, mesh=mesh, in_specs=in_specs, out_specs=out_specs, check_vma=False)
```

profile of v0, /device:TPU:13, one launch (start us, length us, event | category | flops | bytes accessed | tf_op | source)
XLA Modules:
  0.0 1255.8 jit_solution(2749102782969491984)
XLA Ops:
  12.1 15.5 %scatter_custom_fusion.1 = s32[5120]{0:T(1024)S(1)} fusion(s32[4096]{0:T(1024)S(1)} %reshape.262, s32[4096]{0:T(1024)S(1)} %reshape.264, s32[]{:T(128)} %constant.23.clone.1), kind=kCustom, calls=%fused_computation.51 | custom fusion | bytes 20484
  27.9 5.8 gather_fusion.1
  33.6 55.8 %all_to_all.51 = bf16[16,80,1792]{2,1,0:T(8,128)(2,1)S(1)} all-to-all(bf16[16,80,1792]{2,1,0:T(8,128)(2,1)} %bitcast.71), channel_id=1, replica_groups=mesh['groups'=2,'expert'=4,'seq'=4] {'expert'}, dimensions={0} | all-to-all | bytes 9175040 | tf_op jit(solution)/shard_map/all_to_all | solution.py:49
  89.5 2.7 copy.59
  93.2 5.8 gather_fusion
  99.0 56.9 %all_to_all.52 = bf16[16,80,1792]{2,1,0:T(8,128)(2,1)S(1)} all-to-all(bf16[16,80,1792]{2,1,0:T(8,128)(2,1)} %bitcast.70), channel_id=1, replica_groups=mesh['groups'=2,'expert'=4,'seq'=4] {'expert'}, dimensions={0} | all-to-all | bytes 9175040 | tf_op jit(solution)/shard_map/all_to_all | solution.py:50
  160.0 15.8 %scatter_custom_fusion = f32[5120]{0:T(1024)S(1)} fusion(s32[4096]{0:T(1024)S(1)} %reshape.256, f32[4096]{0:T(1024)S(1)} %reshape.258, f32[]{:T(128)} %constant.14.clone.1), kind=kCustom, calls=%fused_computation.53 | custom fusion | bytes 20484
  175.9 15.3 %constant_dynamic-update-slice_fusion.1 = bf16[4,7168,512]{2,1,0:T(8,128)(2,1)} fusion(bf16[4,7168,256]{2,1,0:T(8,128)(2,1)} %param.11), kind=kLoop, calls=%fused_computation.69 | loop fusion | bytes 29360128
  191.3 6.1 constant_dynamic-update-slice_fusion
  197.4 206.6 %all-gather.5.cloned.1.call-done = bf16[4,320,7168]{2,1,0:T(8,128)(2,1)} async-done(((bf16[4,80,7168]{2,1,0:T(8,128)(2,1)}), bf16[4,320,7168]{2,1,0:T(8,128)(2,1)}) %all-gather.5.cloned.1.call-update) | async-done | bytes 18350096 | tf_op jit(solution)/shard_map/all_gather | solution.py:53
  404.0 22.5 %fusion.10 = f32[4,320,512]{2,1,0:T(8,128)S(1)} fusion(bf16[4,320,7168]{2,1,0:T(8,128)(2,1)} %all-gather.5.cloned.1.call-done, bf16[4,7168,512]{2,1,0:T(8,128)(2,1)} %constant_dynamic-update-slice_fusion), kind=kOutput, calls=%fused_computation.79 | convolution fusion | flops 9395240960 | bytes 50331648 | tf_op jit(solution)/shard_map/ezd,edh->ezh/dot_general | solution.py:57
  426.5 291.8 %all-gather.3.cloned.1.call-done = bf16[4,320,7168]{2,1,0:T(8,128)(2,1)} async-done(((bf16[4,80,7168]{2,1,0:T(8,128)(2,1)}), bf16[4,320,7168]{2,1,0:T(8,128)(2,1)}) %all-gather.3.cloned.1.call-update) | async-done | bytes 18350096 | tf_op jit(solution)/shard_map/all_gather | solution.py:54
  718.3 14.1 %multiply_convert_fusion.2 = (bf16[4,320,256]{2,1,0:T(8,128)(2,1)S(1)}, bf16[4,320,256]{2,1,0:T(8,128)(2,1)}, bf16[4,320]{1,0:T(4,128)(2,1)S(1)}) fusion(f32[4,320,512]{2,1,0:T(8,128)S(1)} %fusion.10, f32[4,320]{1,0:T(4,128)S(1)} %constant_dynamic-slice_fusion.1, bf16[4,320,7168]{2,1,0:T(8,128)(2,1)} %all-gather.3.cloned.1.call-done, ...), kind=kOutput, calls=%fused_computation.22 | convolution fusion | flops 4703517696 | bytes 36969984 | tf_op jit(solution)/shard_map/ezd,ehd->ezh/dot_general | solution.py:64
  732.4 19.9 %convolution_convert_fusion.1 = bf16[4,320,7168]{2,1,0:T(8,128)(2,1)} fusion(bf16[4,7168,512]{2,1,0:T(8,128)(2,1)} %constant_dynamic-update-slice_fusion, bf16[4,320,256]{2,1,0:T(8,128)(2,1)} %get-tuple-element.18, bf16[4,320,256]{2,1,0:T(8,128)(2,1)S(1)} %get-tuple-element.17), kind=kOutput, calls=%fused_computation.14 | convolution fusion | flops 9407037440 | bytes 49020928 | tf_op jit(solution)/shard_map/ezh,edh->ezd/dot_general | solution.py:81
  752.3 33.2 %copy.52 = bf16[4,320,7168]{1,0,2:T(4,128)(2,1)} copy(bf16[4,320,7168]{2,1,0:T(8,128)(2,1)} %convolution_convert_fusion.1) | data formatting | bytes 36700160 | tf_op jit(solution)/shard_map/convert_element_type | solution.py:87
  785.5 8.7 all-to-all-start.2
  799.2 9.6 all-reduce.2
  809.5 33.5 %gather_fusion.10 = f32[4096]{0:T(1024)S(1)} fusion(f32[4,80]{1,0:T(4,128)S(1)} %bitcast_convert_fusion, s32[4096]{0:T(1024)S(1)} %reshape.250), kind=kCustom, calls=%fused_computation.10 | custom fusion | bytes 65536 | tf_op jit(solution)/shard_map/gather | solution.py:111
  844.0 195.2 %psum.7 = f32[128,8]{1,0:T(8,128)S(1)} all-reduce(f32[128,8]{1,0:T(8,128)S(1)} %select_reduce_fusion), channel_id=1, replica_groups=mesh['groups'=2,'expert'=4,'seq'=4] {'expert'}, use_global_device_ids=true, to_apply=%region_9.10 | all-reduce | flops 1024 | bytes 8192 | tf_op jit(solution)/shard_map/psum | solution.py:113
  1039.9 22.5 %convolution_convert_fusion = bf16[4,7168,512]{2,1,0:T(8,128)(2,1)} fusion(bf16[4,320,7168]{2,1,0:T(8,128)(2,1)} %all-gather.5.cloned.1.call-done, bf16[4,320,256]{2,1,0:T(8,128)(2,1)S(1)} %copy-done.22, bf16[4,320,256]{2,1,0:T(8,128)(2,1)S(1)} %copy-done.21), kind=kOutput, calls=%fused_computation.13 | convolution fusion | flops 9412542464 | bytes 49020928 | tf_op jit(solution)/shard_map/ezd,ezh->edh/dot_general | solution.py:76
  1062.4 32.4 %copy.53 = bf16[4,320,4,1792]{3,1,0,2:T(8,128)(2,1)} copy(bf16[4,320,4,1792]{1,0,3,2:T(4,128)(2,1)} %bitcast.10) | data formatting | bytes 36700160 | tf_op jit(solution)/shard_map/all_to_all | solution.py:86
  1094.9 12.5 gather_fusion.9
  1107.4 13.5 %gather_fusion.8 = bf16[512,1792]{1,0:T(8,128)(2,1)} fusion(bf16[5120,1792]{1,0:T(8,128)(2,1)} %bitcast.59, s32[1024]{0:T(1024)S(1)} %copy-done.8), kind=kCustom, calls=%fused_computation.8 | custom fusion | bytes 3672064 | tf_op jit(solution)/shard_map/gather | solution.py:96
  1120.9 13.3 %gather_fusion.7 = bf16[512,1792]{1,0:T(8,128)(2,1)} fusion(bf16[5120,1792]{1,0:T(8,128)(2,1)} %bitcast.60, s32[1024]{0:T(1024)S(1)} %copy-done.12), kind=kCustom, calls=%fused_computation.7 | custom fusion | bytes 3672064 | tf_op jit(solution)/shard_map/gather | solution.py:96
  1134.2 13.5 %gather_fusion.6 = bf16[512,1792]{1,0:T(8,128)(2,1)} fusion(bf16[5120,1792]{1,0:T(8,128)(2,1)} %bitcast.61, s32[1024]{0:T(1024)S(1)} %copy-done.9), kind=kCustom, calls=%fused_computation.6 | custom fusion | bytes 3672064 | tf_op jit(solution)/shard_map/gather | solution.py:96
  1147.8 13.4 %gather_fusion.5 = bf16[512,1792]{1,0:T(8,128)(2,1)} fusion(bf16[5120,1792]{1,0:T(8,128)(2,1)} %bitcast.62, s32[1024]{0:T(1024)S(1)} %copy-done.13), kind=kCustom, calls=%fused_computation.5 | custom fusion | bytes 3672064 | tf_op jit(solution)/shard_map/gather | solution.py:96
  1161.2 13.3 %gather_fusion.4 = bf16[512,1792]{1,0:T(8,128)(2,1)} fusion(bf16[5120,1792]{1,0:T(8,128)(2,1)} %bitcast.63, s32[1024]{0:T(1024)S(1)} %copy-done.10), kind=kCustom, calls=%fused_computation.4 | custom fusion | bytes 3672064 | tf_op jit(solution)/shard_map/gather | solution.py:96
  1174.5 13.6 %gather_fusion.3 = bf16[512,1792]{1,0:T(8,128)(2,1)} fusion(bf16[5120,1792]{1,0:T(8,128)(2,1)} %bitcast.64, s32[1024]{0:T(1024)S(1)} %copy-done.15), kind=kCustom, calls=%fused_computation.3 | custom fusion | bytes 3672064 | tf_op jit(solution)/shard_map/gather | solution.py:96
  1188.1 13.4 %gather_fusion.2 = bf16[512,1792]{1,0:T(8,128)(2,1)} fusion(bf16[5120,1792]{1,0:T(8,128)(2,1)} %bitcast.65, s32[1024]{0:T(1024)S(1)} %copy-done.14), kind=kCustom, calls=%fused_computation.2 | custom fusion | bytes 3672064 | tf_op jit(solution)/shard_map/gather | solution.py:96
  1201.5 7.8 add_convert_fusion
  1209.3 18.0 %convolution_convert_fusion.2 = bf16[4,256,7168]{2,1,0:T(8,128)(2,1)} fusion(bf16[4,320,7168]{2,1,0:T(8,128)(2,1)} %all-gather.3.cloned.1.call-done, f32[4,320]{1,0:T(4,128)S(1)} %copy-done.6, f32[4,320,512]{2,1,0:T(8,128)} %copy-done), kind=kOutput, calls=%fused_computation.15 | convolution fusion | flops 4707254272 | bytes 35656704 | tf_op jit(solution)/shard_map/ezh,ezd->ehd/dot_general | solution.py:73
  1227.3 21.6 %fusion.9 = (bf16[4,7168,256]{2,1,0:T(8,128)(2,1)}, bf16[4,7168,256]{2,1,0:T(8,128)(2,1)}) fusion(bf16[4,7168,512]{2,1,0:T(8,128)(2,1)} %convolution_convert_fusion), kind=kLoop, calls=%fused_computation.78 | loop fusion | bytes 58720256 | tf_op jit(solution)/shard_map/slice | solution.py:80
  (116 shorter events, 17.6 us)
Async XLA Ops:
  7.2 20.6 %copy-start.1 = (bf16[128,1792]{1,0:T(8,128)(2,1)S(1)}, bf16[128,1792]{1,0:T(8,128)(2,1)}, u32[]{:S(2)}) copy-start(bf16[128,1792]{1,0:T(8,128)(2,1)} %param.7) | copy-start | bytes 1376260
  7.2 396.9 %all-gather.5.cloned.1.call-start = ((), (), s32[]{:S(2)}) async-start(), calls=%async_computation.5 | async-start | bytes 22937600 | tf_op jit(solution)/shard_map/all_gather | solution.py:53
  92.2 1.0 copy-start.2
  92.2 626.1 %all-gather.3.cloned.1.call-start = ((), (), s32[]{:S(2)}) async-start(), calls=%async_computation.4 | async-start | bytes 22937600 | tf_op jit(solution)/shard_map/all_gather | solution.py:54
  158.6 0.7 copy-start.17
  158.6 0.7 copy-start.16
  158.6 1.1 copy-start.7
  158.6 32.6 %slice-start = ((s8[14680064]{0:T(1024)(128)(4,1)}), s8[2097152]{0:T(1024)(128)(4,1)S(1)}, s32[]{:S(2)}) async-start(s8[14680064]{0:T(1024)(128)(4,1)} %bitcast.72), calls=%async_computation.7 | async-start | bytes 4194304
  175.9 542.4 %copy-start.5 = (f32[4,320]{1,0:T(4,128)}, f32[4,320]{1,0:T(4,128)S(1)}, u32[]{:S(2)}) copy-start(f32[4,320]{1,0:T(4,128)S(1)} %constant_dynamic-slice_fusion.1) | copy-start | bytes 15364
  175.9 15.4 %slice-start.1 = ((s8[14680064]{0:T(1024)(128)(4,1)}), s8[4194304]{0:T(1024)(128)(4,1)S(1)}, s32[]{:S(2)}) async-start(s8[14680064]{0:T(1024)(128)(4,1)} %bitcast.72), calls=%async_computation.8 | async-start | bytes 8388608
  175.9 15.4 %slice-start.2 = ((s8[14680064]{0:T(1024)(128)(4,1)}), s8[4194304]{0:T(1024)(128)(4,1)S(1)}, s32[]{:S(2)}) async-start(s8[14680064]{0:T(1024)(128)(4,1)} %bitcast.72), calls=%async_computation.9 | async-start | bytes 8388608
  175.9 15.4 %slice-start.3 = ((s8[14680064]{0:T(1024)(128)(4,1)}), s8[4194304]{0:T(1024)(128)(4,1)S(1)}, s32[]{:S(2)}) async-start(s8[14680064]{0:T(1024)(128)(4,1)} %bitcast.72), calls=%async_computation.10 | async-start | bytes 8388608
  426.5 305.8 %copy-start = (f32[4,320,512]{2,1,0:T(8,128)}, f32[4,320,512]{2,1,0:T(8,128)S(1)}, u32[]{:S(2)}) copy-start(f32[4,320,512]{2,1,0:T(8,128)S(1)} %fusion.10) | copy-start | bytes 7864324
  732.4 19.9 %copy-start.20 = (bf16[4,320,256]{2,1,0:T(8,128)(2,1)}, bf16[4,320,256]{2,1,0:T(8,128)(2,1)S(1)}, u32[]{:S(2)}) copy-start(bf16[4,320,256]{2,1,0:T(8,128)(2,1)S(1)} %get-tuple-element.17) | copy-start | bytes 1966084
  785.5 9.3 copy-start.3
  785.5 10.0 copy-start.19
  785.5 277.0 %all-to-all-start.2 = ((bf16[4,320,7168]{1,0,2:T(4,128)(2,1)}), bf16[4,320,7168]{1,0,2:T(4,128)(2,1)}, u32[]{:S(2)}, u32[]{:S(2)}) async-start(bf16[4,320,7168]{1,0,2:T(4,128)(2,1)} %copy.52), calls=%async_computation.2 | async-start | bytes 44040192 | tf_op jit(solution)/shard_map/all_to_all | solution.py:86
  794.1 454.7 %reduce-scatter.2.cloned.1.call-start = ((), (), s32[]{:S(2)}) async-start(), calls=%async_computation.6 | async-start | bytes 2293760 | tf_op jit(solution)/shard_map/reduce_scatter | solution.py:99
  809.5 34.1 %copy-start.4 = (s32[128,8]{1,0:T(8,128)S(1)}, s32[128,8]{1,0:T(8,128)}, u32[]{:S(2)}) copy-start(s32[128,8]{1,0:T(8,128)} %copy.54) | copy-start | bytes 12292
  809.5 34.1 %copy-start.18 = (s32[4]{0:T(128)S(1)}, s32[4]{0:T(128)}, u32[]{:S(2)}) copy-start(s32[4]{0:T(128)} %iota_add_fusion) | copy-start | bytes 52
  809.5 230.4 %copy-start.21 = (bf16[4,320,256]{2,1,0:T(8,128)(2,1)S(1)}, bf16[4,320,256]{2,1,0:T(8,128)(2,1)}, u32[]{:S(2)}) copy-start(bf16[4,320,256]{2,1,0:T(8,128)(2,1)} %copy-done.20) | copy-start | bytes 1966084
  809.5 230.4 %copy-start.22 = (bf16[4,320,256]{2,1,0:T(8,128)(2,1)S(1)}, bf16[4,320,256]{2,1,0:T(8,128)(2,1)}, u32[]{:S(2)}) copy-start(bf16[4,320,256]{2,1,0:T(8,128)(2,1)} %get-tuple-element.18) | copy-start | bytes 1966084
  1062.4 32.4 %copy-start.11 = (s32[1024]{0:T(1024)S(1)}, s32[1024]{0:T(1024)}, u32[]{:S(2)}) copy-start(s32[1024]{0:T(1024)} %get-tuple-element.31) | copy-start | bytes 12292
  1094.9 12.5 copy-start.8
  1107.4 13.5 %copy-start.12 = (s32[1024]{0:T(1024)S(1)}, s32[1024]{0:T(1024)}, u32[]{:S(2)}) copy-start(s32[1024]{0:T(1024)} %get-tuple-element.33) | copy-start | bytes 12292
  1120.9 13.3 %copy-start.9 = (s32[1024]{0:T(1024)S(1)}, s32[1024]{0:T(1024)}, u32[]{:S(2)}) copy-start(s32[1024]{0:T(1024)} %get-tuple-element.34) | copy-start | bytes 12292
  1134.2 13.6 %copy-start.13 = (s32[1024]{0:T(1024)S(1)}, s32[1024]{0:T(1024)}, u32[]{:S(2)}) copy-start(s32[1024]{0:T(1024)} %get-tuple-element.35) | copy-start | bytes 12292
  1147.8 13.4 %copy-start.10 = (s32[1024]{0:T(1024)S(1)}, s32[1024]{0:T(1024)}, u32[]{:S(2)}) copy-start(s32[1024]{0:T(1024)} %get-tuple-element.36) | copy-start | bytes 12292
  1161.2 13.3 %copy-start.15 = (s32[1024]{0:T(1024)S(1)}, s32[1024]{0:T(1024)}, u32[]{:S(2)}) copy-start(s32[1024]{0:T(1024)} %get-tuple-element.37) | copy-start | bytes 12292
  1174.5 13.6 %copy-start.14 = (s32[1024]{0:T(1024)S(1)}, s32[1024]{0:T(1024)}, u32[]{:S(2)}) copy-start(s32[1024]{0:T(1024)} %get-tuple-element.38) | copy-start | bytes 12292
  1201.5 7.8 copy-start.6
Sparse Core Ops, SparseCore 0:
  92.3 311.6 all-gather.4
  406.2 312.0 all-gather.2
  1209.4 38.4 reduce-scatter.1
where the time goes:
time: 1270 us; the launch traced here: 1260 us
  waiting for transfers between devices  498 us (39%)
  blocking collectives  318 us (25%)
  local copies, waits for them, and re-layouts  303 us (24%)
  matrix products  96.9 us (8%)
  other arithmetic  16.3 us (1%)
  between operations  14.6 us (1%)
    all_gather x1, waiting for transfers between devices, body(): lax.all_gather(local_grads, 'seq', axis=1, tiled=True)  292 us
    all_gather x1, waiting for transfers between devices, body(): lax.all_gather(local_tokens, 'seq', axis=1, tiled=True)  207 us
    psum x1, blocking collectives, body(): gate_grad = lax.psum(gate_part, 'expert')  195 us
    gather x8, local copies, waits for them, and re-layouts, body(): token_sum = token_sum + flat_rows[row_index[:, column]].astype(jnp.float32)  107 us
    all_to_all x1, blocking collectives, body(): lax.all_to_all(send_grads, 'expert', split_axis=0, concat_axis=2, tiled=T...  56.9 us
    all_to_all x1, blocking collectives, body(): lax.all_to_all(send_tokens, 'expert', split_axis=0, concat_axis=2, tiled=...  55.8 us
    unnamed x64, local copies, waits for them, and re-layouts  50.2 us
    gather x2, local copies, waits for them, and re-layouts, body(): picked = own_scores[expert_slots, own_slots[:, :, None]]  34.1 us
  transfers between devices with their start and end apart: 4, of which 2 were waited for; matrix products, arithmetic and copies ran while one was open for 14% of the time, Pallas kernels for 0%

commit v1 on v0

v1 whole, which is shorter than its diff:
```python
import functools

import jax
import jax.numpy as jnp
from jax import lax
from jax.experimental import pallas as pl
from jax.experimental.pallas import tpu as pltpu
from jax.sharding import PartitionSpec as P

BOTH = ("expert", "seq")
VMEM_BYTES = 56 * 1024 * 1024
BF16 = jnp.bfloat16
F32 = jnp.float32


def params(dims):
    return pltpu.CompilerParams(
        vmem_limit_bytes=VMEM_BYTES, dimension_semantics=("arbitrary",) * dims
    )


def cost(flops, moved):
    return pl.CostEstimate(flops=int(flops), bytes_accessed=int(moved), transcendentals=0)


def dot_nn(a, b):
    return lax.dot_general(a, b, (((1,), (0,)), ((), ())), preferred_element_type=F32)


def dot_nt(a, b):
    return lax.dot_general(a, b, (((1,), (1,)), ((), ())), preferred_element_type=F32)


def pre_kernel(x_ref, gate_ref, up_ref, pre_gate_ref, pre_up_ref):
    c, block = pl.program_id(0), pl.program_id(1)
    group = gate_ref.shape[0]
    for i in range(group):
        e = block * group + i
        new_gate = dot_nn(x_ref[0], gate_ref[i])
        new_up = dot_nn(x_ref[0], up_ref[i])

        @pl.when(c == 0)
        def _():
            pre_gate_ref[e] = new_gate
            pre_up_ref[e] = new_up

        @pl.when(c > 0)
        def _():
            pre_gate_ref[e] += new_gate
            pre_up_ref[e] += new_up


def pre_products(x_all, w_gate, w_up):
    chunks, rows, features = x_all.shape
    experts, depth, width = w_gate.shape
    group = min(2, experts)
    weight_spec = pl.BlockSpec((group, features, width), lambda c, b: (b, c, 0))
    whole = pl.BlockSpec((experts, rows, width), lambda c, b: (0, 0, 0))
    out = jax.ShapeDtypeStruct((experts, rows, width), F32)
    return pl.pallas_call(
        pre_kernel,
        grid=(chunks, experts // group),
        in_specs=[
            pl.BlockSpec((1, rows, features), lambda c, b: (c, 0, 0)),
            weight_spec,
            weight_spec,
        ],
        out_specs=[whole, whole],
        out_shape=[out, out],
        compiler_params=params(2),
        cost_estimate=cost(
            4 * rows * depth * width * experts,
            2 * rows * depth + 4 * experts * depth * width + 8 * experts * rows * width,
        ),
        name="pre_products",
    )(x_all, w_gate, w_up)


def back_kernel(
    g_ref, down_ref, pre_gate_ref, pre_up_ref, weight_ref,
    grads_ref, scaled_act_ref, scores_ref, back_ref,
):
    c, block = pl.program_id(0), pl.program_id(1)
    last = pl.num_programs(0) - 1
    group, width = down_ref.shape[0], down_ref.shape[1]
    experts = back_ref.shape[0]
    for i in range(group):
        e = block * group + i
        new = dot_nt(g_ref[0], down_ref[i])

        @pl.when(c == 0)
        def _():
            back_ref[e] = new

        @pl.when(c > 0)
        def _():
            back_ref[e] += new

    @pl.when((c == last) & (block == pl.num_programs(1) - 1))
    def _():
        for e in range(experts):
            pre_gate = pre_gate_ref[e]
            pre_up = pre_up_ref[e]
            back = back_ref[e]
            r = weight_ref[:, e : e + 1]
            sig = jax.nn.sigmoid(pre_gate)
            silu = pre_gate * sig
            act = silu * pre_up
            scores_ref[:, e : e + 1] = jnp.sum(act * back, axis=1, keepdims=True)
            scaled = r * back
            grads_ref[:, e * width : (e + 1) * width] = (
                scaled * pre_up * sig * (1.0 + pre_gate * (1.0 - sig))
            ).astype(BF16)
            at = (experts + e) * width
            grads_ref[:, at : at + width] = (scaled * silu).astype(BF16)
            scaled_act_ref[e * width : (e + 1) * width, :] = (r * act).T.astype(BF16)


def back_products(g_all, w_down, pre_gate, pre_up, weight):
    chunks, rows, features = g_all.shape
    experts, width, depth = w_down.shape
    group = min(2, experts)
    whole = pl.BlockSpec((experts, rows, width), lambda c, b: (0, 0, 0))
    return pl.pallas_call(
        back_kernel,
        grid=(chunks, experts // group),
        in_specs=[
            pl.BlockSpec((1, rows, features), lambda c, b: (c, 0, 0)),
            pl.BlockSpec((group, width, features), lambda c, b: (b, 0, c)),
            whole,
            whole,
            pl.BlockSpec((rows, experts), lambda c, b: (0, 0)),
        ],
        out_specs=[
            pl.BlockSpec((rows, 2 * experts * width), lambda c, b: (0, 0)),
            pl.BlockSpec((experts * width, rows), lambda c, b: (0, 0)),
            pl.BlockSpec((rows, experts), lambda c, b: (0, 0)),
        ],
        out_shape=[
            jax.ShapeDtypeStruct((rows, 2 * experts * width), BF16),
            jax.ShapeDtypeStruct((experts * width, rows), BF16),
            jax.ShapeDtypeStruct((rows, experts), F32),
        ],
        scratch_shapes=[pltpu.VMEM((experts, rows, width), F32)],
        compiler_params=params(2),
        cost_estimate=cost(
            2 * rows * depth * width * experts,
            2 * rows * depth + 2 * experts * depth * width + 8 * experts * rows * width,
        ),
        name="back_products",
    )(g_all, w_down, pre_gate, pre_up, weight)


def row_kernel(grads_ref, gate_ref, up_ref, out_ref):
    experts, _, width = gate_ref.shape
    total = None
    for e in range(experts):
        for half, ref in enumerate((gate_ref, up_ref)):
            at = (half * experts + e) * width
            term = dot_nt(grads_ref[:, at : at + width], ref[e])
            total = term if total is None else total + term
    out_ref[0] = total.astype(BF16)


def row_products(grads, w_gate, w_up, chunks, steps, first, count):
    rows = grads.shape[0]
    experts, depth, width = w_gate.shape
    features = depth // chunks
    cut = count // steps
    weight_spec = pl.BlockSpec(
        (experts, cut, width), lambda c, n: (0, c * (features // cut) + first // cut + n, 0)
    )
    return pl.pallas_call(
        row_kernel,
        grid=(chunks, steps),
        in_specs=[
            pl.BlockSpec(grads.shape, lambda c, n: (0, 0)),
            weight_spec,
            weight_spec,
        ],
        out_specs=pl.BlockSpec((1, rows, cut), lambda c, n: (c, 0, n)),
        out_shape=jax.ShapeDtypeStruct((chunks, rows, count), BF16),
        compiler_params=params(2),
        cost_estimate=cost(
            4 * rows * chunks * count * width * experts,
            2 * rows * chunks * count + 4 * experts * chunks * count * width,
        ),
        name="row_products",
    )(grads, w_gate, w_up)


def weight_kernel(x_ref, g_ref, grads_ref, act_ref, gate_ref, up_ref, down_ref):
    experts, _, width = gate_ref.shape
    x_t = x_ref[0].T
    for e in range(experts):
        gate_ref[e] = dot_nn(x_t, grads_ref[:, e * width : (e + 1) * width]).astype(BF16)
        at = (experts + e) * width
        up_ref[e] = dot_nn(x_t, grads_ref[:, at : at + width]).astype(BF16)
        down_ref[e] = dot_nn(act_ref[e * width : (e + 1) * width, :], g_ref[0]).astype(BF16)


def weight_products(x_all, g_all, grads, act_t, experts, steps):
    chunks, rows, features = x_all.shape
    width = act_t.shape[0] // experts
    depth = chunks * features
    cut = features // steps
    token_spec = pl.BlockSpec((1, rows, cut), lambda c, n: (c, 0, n))
    tall = pl.BlockSpec((experts, cut, width), lambda c, n: (0, c * steps + n, 0))
    return pl.pallas_call(
        weight_kernel,
        grid=(chunks, steps),
        in_specs=[
            token_spec,
            token_spec,
            pl.BlockSpec(grads.shape, lambda c, n: (0, 0)),
            pl.BlockSpec(act_t.shape, lambda c, n: (0, 0)),
        ],
        out_specs=[
            tall,
            tall,
            pl.BlockSpec((experts, width, cut), lambda c, n: (0, 0, c * steps + n)),
        ],
        out_shape=[
            jax.ShapeDtypeStruct((experts, depth, width), BF16),
            jax.ShapeDtypeStruct((experts, depth, width), BF16),
            jax.ShapeDtypeStruct((experts, width, depth), BF16),
        ],
        compiler_params=params(2),
        cost_estimate=cost(
            6 * rows * depth * width * experts,
            4 * rows * depth + 6 * experts * depth * width,
        ),
        name="weight_products",
    )(x_all, g_all, grads, act_t)


def body(tokens, out_grad, routes, route_weights, w_gate, w_up, w_down):
    shards = lax.axis_size("seq")
    feature_shards = lax.axis_size("expert")
    tok_rows, features = tokens.shape
    rows = shards * tok_rows
    local_experts, depth, width = w_gate.shape
    first_expert = lax.axis_index("expert") * local_experts

    x_all = lax.all_gather(tokens, BOTH, axis=0, tiled=False).reshape(
        feature_shards, rows, features
    )
    g_all = lax.all_gather(out_grad, BOTH, axis=0, tiled=False).reshape(
        feature_shards, rows, features
    )
    local_ids = first_expert + jnp.arange(local_experts, dtype=jnp.int32)
    hit = routes[:, :, None] == local_ids[None, None, :]
    weight = jnp.sum(jnp.where(hit, route_weights[:, :, None], 0.0), axis=1)

    if features % 256 == 0:
        pre_gate, pre_up = pre_products(x_all, w_gate, w_up)
        grads, act_t, scores = back_products(g_all, w_down, pre_gate, pre_up, weight)
        part = row_products(grads, w_gate, w_up, feature_shards, 2, 0, features)
        weight_grads = lambda: weight_products(x_all, g_all, grads, act_t, local_experts, 2)
    else:
        part, scores, weight_grads = plain(x_all, g_all, weight, w_gate, w_up, w_down)

    part = part.reshape(feature_shards * shards, tok_rows, features)
    token_grad = lax.psum_scatter(part, BOTH, scatter_dimension=0, tiled=True)[0]
    picked = jnp.sum(jnp.where(hit, scores[:, None, :], 0.0), axis=2)
    gate_grad = lax.psum(lax.psum_scatter(picked, "seq", scatter_dimension=0, tiled=True), "expert")
    grad_gate, grad_up, grad_down = weight_grads()
    return token_grad, grad_gate, grad_up, grad_down, gate_grad


def plain(x_all, g_all, weight, w_gate, w_up, w_down):
    chunks, rows, features = x_all.shape
    experts, depth, width = w_gate.shape
    weight = weight.T[:, :, None]
    gate4 = w_gate.reshape(experts, chunks, features, width)
    up4 = w_up.reshape(experts, chunks, features, width)
    down4 = w_down.reshape(experts, width, chunks, features)
    einsum = functools.partial(jnp.einsum, preferred_element_type=F32)
    pre_gate = einsum("crf,ecfh->erh", x_all, gate4)
    pre_up = einsum("crf,ecfh->erh", x_all, up4)
    back = einsum("crf,ehcf->erh", g_all, down4)
    sig = jax.nn.sigmoid(pre_gate)
    act = pre_gate * sig * pre_up
    scores = jnp.sum(act * back, axis=2).T
    scaled = weight * back
    up_grad = (scaled * pre_gate * sig).astype(BF16)
    pre_grad = (scaled * pre_up * sig * (1.0 + pre_gate * (1.0 - sig))).astype(BF16)
    scaled_act = (weight * act).astype(BF16)
    part = einsum("erh,ecfh->crf", pre_grad, gate4) + einsum("erh,ecfh->crf", up_grad, up4)

    def weight_grads():
        return (
            einsum("crf,erh->ecfh", x_all, pre_grad).astype(BF16).reshape(w_gate.shape),
            einsum("crf,erh->ecfh", x_all, up_grad).astype(BF16).reshape(w_up.shape),
            einsum("erh,crf->ehcf", scaled_act, g_all).astype(BF16).reshape(w_down.shape),
        )

    return part.astype(BF16), scores, weight_grads


def solution(mesh):
    in_specs = (
        P(("groups", "seq"), "expert"),
        P(("groups", "seq"), "expert"),
        P("groups", None),
        P("groups", None),
        P("expert", None, "seq"),
        P("expert", None, "seq"),
        P("expert", "seq", None),
    )
    out_specs = (
        P(("groups", "seq"), "expert"),
        P(("groups", "expert"), None, "seq"),
        P(("groups", "expert"), None, "seq"),
        P(("groups", "expert"), "seq", None),
        P(("groups", "seq"), None),
    )
    return jax.shard_map(body, mesh=mesh, in_specs=in_specs, out_specs=out_specs, check_vma=False)
```

time: 1270 us -> 298 us (0.23)
  waiting for transfers between devices: 498 us -> 168 us
  blocking collectives: 318 us -> 6.15 us
  local copies, waits for them, and re-layouts: 303 us -> 1.92 us
  Pallas kernels: 0 us -> 105 us
  matrix products: 96.9 us -> 0 us
  other arithmetic: 16.3 us -> 1.52 us
    all_gather x2, waiting for transfers between devices: 498 us -> 114 us  [the longest x1 69.5 us: body(): lax.all_gather(tokens, BOTH, axis=0, tiled=False)]
    psum x1, blocking collectives: 195 us -> 6.15 us  [body(): lax.psum(lax.psum_scatter(picked, 'seq', scatter_dimension=0, tiled=True)...]
    gather x12 -> x0, local copies, waits for them, and re-layouts: 152 us -> none  [the longest x8 107 us: body(): token_sum = token_sum + flat_rows[row_index[:, column]].astype(jnp.float32)]
    all_to_all x2 -> x0, blocking collectives: 113 us -> none  [the longest x1 56.9 us: body(): lax.all_to_all(send_grads, 'expert', split_axis=0, concat_axis=2, tiled=T...]
    pallas_call x0 -> x4, Pallas kernels: none -> 105 us  [the longest x1 31.2 us: weight_products(): pl.pallas_call(weight_kernel, grid=(chunks, steps), in_specs=[token_spec,...]
    dot_general x5 -> x0, matrix products: 96.9 us -> none  [the longest x1 22.5 us: body(): jnp.einsum('ezd,ezh->edh', rows_in, joined_grads, preferred_element_type=...]
    reduce_scatter x1 -> x2, waiting for transfers between devices: 0.01 us -> 53 us  [the longest x1 53 us: body(): lax.psum_scatter(part, BOTH, scatter_dimension=0, tiled=True)[0]]
    unnamed x64 -> x2, local copies, waits for them, and re-layouts: 50.2 us -> 0.01 us
  transfers between devices with their start and end apart: 4 -> 4, of which waited for: 2 -> 3; matrix products, arithmetic and copies ran while one was open for 14% -> 1% of each run, Pallas kernels for 0% -> 27%
where the time goes in v1:
time: 298 us; the launch traced here: 296 us
  waiting for transfers between devices  168 us (56%)
  Pallas kernels  105 us (35%)
  between operations  13.8 us (5%)
  blocking collectives  6.15 us (2%)
    all_gather x1, waiting for transfers between devices, body(): lax.all_gather(tokens, BOTH, axis=0, tiled=False)  69.5 us
    reduce_scatter x1, waiting for transfers between devices, body(): lax.psum_scatter(part, BOTH, scatter_dimension=0, tiled=True)[0]  53 us
    all_gather x1, waiting for transfers between devices, body(): lax.all_gather(out_grad, BOTH, axis=0, tiled=False)  44.4 us
    pallas_call x1, Pallas kernels, weight_products(): pl.pallas_call(weight_kernel, grid=(chunks, steps), in_specs=[token_spec,...  31.2 us
    pallas_call x1, Pallas kernels, back_products(): pl.pallas_call(back_kernel, grid=(chunks, experts // group), in_specs=[pl...  25.8 us
    pallas_call x1, Pallas kernels, pre_products(): pl.pallas_call(pre_kernel, grid=(chunks, experts // group), in_specs=[pl....  24.7 us
    pallas_call x1, Pallas kernels, row_products(): pl.pallas_call(row_kernel, grid=(chunks, steps), in_specs=[pl.BlockSpec(g...  22.9 us
    psum x1, blocking collectives, body(): lax.psum(lax.psum_scatter(picked, 'seq', scatter_dimension=0, tiled=True)...  6.15 us
  transfers between devices with their start and end apart: 4, of which 3 were waited for; matrix products, arithmetic and copies ran while one was open for 1% of the time, Pallas kernels for 27%

profile of v1, /device:TPU:13, one launch (start us, length us, event | category | flops | bytes accessed | tf_op | source)
XLA Modules:
  0.0 296.3 jit_solution(3485604937525001482)
XLA Ops:
  7.2 0.0 all-gather.7.cloned.1.call-start
  7.2 0.7 all-gather.7.cloned.1.call-update
  7.9 0.0 all-gather.5.cloned.1.call-start
  7.9 0.7 all-gather.5.cloned.1.call-update
  8.6 0.0 reduce-scatter.5.cloned.1.call-start
  8.7 0.8 fusion
  9.5 0.9 copy.14.weight_ref
  10.4 69.5 %all-gather.7.cloned.1.call-done = bf16[2048,1792]{1,0:T(8,128)(2,1)} async-done(((bf16[128,1792]{1,0:T(8,128)(2,1)}), bf16[2048,1792]{1,0:T(8,128)(2,1)}) %all-gather.7.cloned.1.call-update) | async-done | bytes 7340048 | tf_op jit(solution)/shard_map/all_gather | solution.py:245
  79.9 24.7 %pre_products.1 = (f32[4,512,256]{2,1,0:T(8,128)}, f32[4,512,256]{2,1,0:T(8,128)}) custom-call(bf16[4,512,1792]{2,1,0:T(8,128)(2,1)} %bitcast.5, bf16[4,7168,256]{2,1,0:T(8,128)(2,1)} %gate_ref.3, bf16[4,7168,256]{2,1,0:T(8,128)(2,1)} %up_ref.3), custom_call_target="tpu_custom_call" | custom-call | flops 15032385536 | bytes 40894464 | tf_op jit(solution)/shard_map/pre_products/pallas_call | solution.py:60
  104.5 0.0 copy-start
  104.5 44.4 %all-gather.5.cloned.1.call-done = bf16[2048,1792]{1,0:T(8,128)(2,1)} async-done(((bf16[128,1792]{1,0:T(8,128)(2,1)}), bf16[2048,1792]{1,0:T(8,128)(2,1)}) %all-gather.5.cloned.1.call-update) | async-done | bytes 7340048 | tf_op jit(solution)/shard_map/all_gather | solution.py:248
  148.9 25.8 %back_products.1 = (bf16[512,2048]{1,0:T(8,128)(2,1)}, bf16[1024,512]{1,0:T(8,128)(2,1)}, f32[512,4]{1,0:T(8,128)}) custom-call(bf16[4,512,1792]{2,1,0:T(8,128)(2,1)} %bitcast.7, bf16[4,256,7168]{2,1,0:T(8,128)(2,1)} %down_ref.1, f32[4,512,256]{2,1,0:T(8,128)} %get-tuple-element.13.pre_gate_ref, f32[4,512,256]{2,1,0:T(8,128)} %get-tuple-element.14.pre_up_ref, ...), custom_call_target="tpu_custom_call" | custom-call | flops 7516192768 | bytes 26214400 | tf_op jit(solution)/shard_map/back_products/pallas_call | solution.py:124
  174.7 1.1 copy.15
  175.8 0.0 copy-done
  175.8 0.7 fusion.1
  176.5 0.0 reduce-scatter.5.cloned.1.call-update
  176.5 0.0 reduce-scatter.3.cloned.1.call-start
  176.6 22.9 %row_products.1 = bf16[4,512,1792]{2,1,0:T(8,128)(2,1)} custom-call(bf16[512,2048]{1,0:T(8,128)(2,1)} %get-tuple-element.15.grads_ref, bf16[4,7168,256]{2,1,0:T(8,128)(2,1)} %gate_ref.3, bf16[4,7168,256]{2,1,0:T(8,128)(2,1)} %up_ref.3), custom_call_target="tpu_custom_call" | custom-call | flops 15032385536 | bytes 36700160 | tf_op jit(solution)/shard_map/row_products/pallas_call | solution.py:173
  199.4 0.0 reduce-scatter.3.cloned.1.call-update
  199.5 31.2 %weight_products.1 = (bf16[4,7168,256]{2,1,0:T(8,128)(2,1)}, bf16[4,7168,256]{2,1,0:T(8,128)(2,1)}, bf16[4,256,7168]{2,1,0:T(8,128)(2,1)}) custom-call(bf16[4,512,1792]{2,1,0:T(8,128)(2,1)} %bitcast.6, bf16[4,512,1792]{2,1,0:T(8,128)(2,1)} %bitcast.8, bf16[512,2048]{1,0:T(8,128)(2,1)} %get-tuple-element.15.grads_ref, bf16[1024,512]{1,0:T(8,128)(2,1)} %get-tuple-element.16.act_ref), custom_call_target="tpu_custom_call" | custom-call | flops 22548578304 | bytes 58720256 | tf_op jit(solution)/shard_map/weight_products/pallas_call | solution.py:209
  230.6 0.0 reduce-scatter.5.cloned.1.call-done
  230.6 6.2 %psum.7 = f32[128,8]{0,1:T(8,128)} all-reduce(f32[128,8]{0,1:T(8,128)} %reduce-scatter.5.cloned.1.call-done), channel_id=1, replica_groups=mesh['groups'=2,'expert'=4,'seq'=4] {'expert'}, use_global_device_ids=true, to_apply=%region_4.5 | all-reduce | flops 1024 | bytes 8192 | tf_op jit(solution)/shard_map/psum | solution.py:266
  236.8 53.0 %reduce-scatter.3.cloned.1.call-done = bf16[1,128,1792]{2,1,0:T(8,128)(2,1)} async-done(((bf16[16,128,1792]{2,1,0:T(8,128)(2,1)}), bf16[1,128,1792]{2,1,0:T(8,128)(2,1)}) %reduce-scatter.3.cloned.1.call-update) | async-done | bytes 458768 | tf_op jit(solution)/shard_map/reduce_scatter | solution.py:264
  (1 shorter events, 0.0 us)
Async XLA Ops:
  7.2 72.7 %all-gather.7.cloned.1.call-start = ((), (), s32[]{:S(2)}) async-start(), calls=%async_computation.5 | async-start | bytes 7798784 | tf_op jit(solution)/shard_map/all_gather | solution.py:245
  7.9 141.0 %all-gather.5.cloned.1.call-start = ((), (), s32[]{:S(2)}) async-start(), calls=%async_computation.4 | async-start | bytes 7798784 | tf_op jit(solution)/shard_map/all_gather | solution.py:248
  8.6 222.0 %reduce-scatter.5.cloned.1.call-start = ((), (), s32[]{:S(2)}) async-start(), calls=%async_computation.3 | async-start | bytes 20480 | tf_op jit(solution)/shard_map/reduce_scatter | solution.py:266
  104.5 71.3 %copy-start = (s32[512,8]{0,1:T(8,128)S(1)}, s32[512,8]{0,1:T(8,128)}, u32[]{:S(2)}) copy-start(s32[512,8]{0,1:T(8,128)} %param.9) | copy-start | bytes 49156
  176.5 113.2 %reduce-scatter.3.cloned.1.call-start = ((), (), s32[]{:S(2)}) async-start(), calls=%async_computation.2 | async-start | bytes 7798784 | tf_op jit(solution)/shard_map/reduce_scatter | solution.py:264
Sparse Core Ops, SparseCore 0:
  10.3 69.5 all-gather.6
  82.2 66.6 all-gather.4
  176.6 12.4 reduce-scatter.4
  199.6 90.1 reduce-scatter.2

commit v2 on v1

--- a/solution.py
+++ b/solution.py
@@ -31,124 +31,226 @@
     return lax.dot_general(a, b, (((1,), (1,)), ((), ())), preferred_element_type=F32)
 
 
-def pre_kernel(x_ref, gate_ref, up_ref, pre_gate_ref, pre_up_ref):
-    c, block = pl.program_id(0), pl.program_id(1)
-    group = gate_ref.shape[0]
-    for i in range(group):
-        e = block * group + i
-        new_gate = dot_nn(x_ref[0], gate_ref[i])
-        new_up = dot_nn(x_ref[0], up_ref[i])
-
-        @pl.when(c == 0)
-        def _():
-            pre_gate_ref[e] = new_gate
-            pre_up_ref[e] = new_up
-
-        @pl.when(c > 0)
-        def _():
-            pre_gate_ref[e] += new_gate
-            pre_up_ref[e] += new_up
-
-
-def pre_products(x_all, w_gate, w_up):
-    chunks, rows, features = x_all.shape
+def forward_kernel(
+    tokens_ref, grad_ref, gate_ref, up_ref, down_ref, weight_ref,
+    x_all_ref, g_all_ref, grads_ref, scaled_act_ref, scores_ref,
+    pre_gate_ref, pre_up_ref, back_ref,
+    z_send, z_recv, x_send, x_recv, s_send, s_recv, local_sem,
+):
+    shards = lax.axis_size("seq")
+    z = lax.axis_index("seq")
+    me = lax.axis_index("expert")
+    sib = me + 1 - 2 * lax.rem(me, 2)
+    partner = lax.rem(me + 2, 4)
+    far = lax.rem(sib + 2, 4)
+    tok_rows, features = tokens_ref.shape
+    experts, _, width = gate_ref.shape
+    own_refs = (tokens_ref, grad_ref)
+    all_refs = (x_all_ref, g_all_ref)
+
+    def place(t, chunk, shard):
+        return all_refs[t].at[chunk, pl.ds(pl.multiple_of(shard * tok_rows, tok_rows), tok_rows)]
+
+    def remote(src, dst, send, recv, device):
+        return pltpu.make_async_remote_copy(
+            src_ref=src, dst_ref=dst, send_sem=send, recv_sem=recv,
+            device_id=device, device_id_type=pl.DeviceIdType.MESH,
+        )
+
+    def source(t, chunk, d):
+        return own_refs[t] if (d == 0 and chunk is me) else place(t, chunk, back_by(d))
+
+    def back_by(d):
+        return lax.rem(z + shards - d, shards)
+
+    def z_copy(t, d):
+        peer = lax.rem(z + d, shards)
+        return remote(own_refs[t], place(t, me, z), z_send.at[t, d], z_recv.at[t, d], {"seq": peer})
+
+    def x_copy(t, d):
+        return remote(
+            source(t, me, d), place(t, me, back_by(d)), x_send.at[t, d], x_recv.at[t, d],
+            {"expert": partner},
+        )
+
+    def s_copy(t, which, d):
+        chunk = (me, partner)[which]
+        at = which * shards + d
+        return remote(
+            source(t, chunk, d), place(t, chunk, back_by(d)), s_send.at[t, at], s_recv.at[t, at],
+            {"expert": sib},
+        )
+
+    def local(t):
+        return pltpu.make_async_copy(own_refs[t], place(t, me, z), local_sem.at[t])
+
+    barrier = pltpu.get_barrier_semaphore()
+    for device in [{"expert": sib}, {"expert": partner}] + [
+        {"seq": lax.rem(z + d, shards)} for d in range(1, shards)
+    ]:
+        pl.semaphore_signal(barrier, inc=1, device_id=device, device_id_type=pl.DeviceIdType.MESH)
+    pl.semaphore_wait(barrier, shards + 1)
+
+    group = 2 if experts % 2 == 0 else 1
+    rows = shards * tok_rows
+
+    def multiply_tokens(chunk, first):
+        def step(x_ref, g_ref, u_ref):
+            block = pl.program_id(0)
+            for i in range(group):
+                e = block * group + i
+                new_gate = dot_nn(x_ref[...], g_ref[i])
+                new_up = dot_nn(x_ref[...], u_ref[i])
+                if first:
+                    pre_gate_ref[e] = new_gate
+                    pre_up_ref[e] = new_up
+                else:
+                    pre_gate_ref[e] += new_gate
+                    pre_up_ref[e] += new_up
+
+        weights = pl.BlockSpec((group, features, width), lambda b: (b, 0, 0))
+        at = pl.ds(pl.multiple_of(chunk * features, features), features)
+        pltpu.emit_pipeline(
+            step,
+            grid=(experts // group,),
+            in_specs=[pl.BlockSpec((rows, features), lambda b: (0, 0)), weights, weights],
+            out_specs=[],
+        )(x_all_ref.at[chunk], gate_ref.at[:, at], up_ref.at[:, at])
+
+    def multiply_grads(chunk, first):
+        def step(g_ref, d_ref):
+            block = pl.program_id(0)
+            for i in range(group):
+                e = block * group + i
+                new = dot_nt(g_ref[...], d_ref[i])
+                if first:
+                    back_ref[e] = new
+                else:
+                    back_ref[e] += new
+
+        at = pl.ds(pl.multiple_of(chunk * features, features), features)
+        pltpu.emit_pipeline(
+            step,
+            grid=(experts // group,),
+            in_specs=[
+                pl.BlockSpec((rows, features), lambda b: (0, 0)),
+                pl.BlockSpec((group, width, features), lambda b: (b, 0, 0)),
+            ],
+            out_specs=[],
+        )(g_all_ref.at[chunk], down_ref.at[:, :, at])
+
+    every = range(shards)
+    others = range(1, shards)
+    for d in others:
+        z_copy(0, d).start()
+    x_copy(0, 0).start()
+    s_copy(0, 0, 0).start()
+    x_copy(1, 0).start()
+    local(0).start()
+    local(1).start()
+    for d in others:
+        z_copy(0, d).wait_recv()
+        x_copy(0, d).start()
+        s_copy(0, 0, d).start()
+    for d in others:
+        z_copy(1, d).start()
+    s_copy(1, 0, 0).start()
+    local(0).wait()
+    local(1).wait()
+    multiply_tokens(me, True)
+    for d in every:
+        s_copy(0, 0, d).wait_recv()
+    multiply_tokens(sib, False)
+    for d in every:
+        x_copy(0, d).wait_recv()
+        s_copy(0, 1, d).start()
+    multiply_tokens(partner, False)
+    for d in every:
+        s_copy(0, 1, d).wait_recv()
+    multiply_tokens(far, False)
+    for d in others:
+        z_copy(1, d).wait_recv()
+        x_copy(1, d).start()
+        s_copy(1, 0, d).start()
+    multiply_grads(me, True)
+    for d in every:
+        s_copy(1, 0, d).wait_recv()
+    multiply_grads(sib, False)
+    for d in every:
+        x_copy(1, d).wait_recv()
+        s_copy(1, 1, d).start()
+    multiply_grads(partner, False)
+    for d in every:
+        s_copy(1, 1, d).wait_recv()
+    multiply_grads(far, False)
+
+    for e in range(experts):
+        pre_gate = pre_gate_ref[e]
+        pre_up = pre_up_ref[e]
+        back = back_ref[e]
+        r = weight_ref[:, e : e + 1]
+        sig = jax.nn.sigmoid(pre_gate)
+        silu = pre_gate * sig
+        act = silu * pre_up
+        scores_ref[:, e : e + 1] = jnp.sum(act * back, axis=1, keepdims=True)
+        scaled = r * back
+        grads_ref[:, e * width : (e + 1) * width] = (
+            scaled * pre_up * sig * (1.0 + pre_gate * (1.0 - sig))
+        ).astype(BF16)
+        at = (experts + e) * width
+        grads_ref[:, at : at + width] = (scaled * silu).astype(BF16)
+        scaled_act_ref[e * width : (e + 1) * width, :] = (r * act).T.astype(BF16)
+
+    for t in range(2):
+        for d in others:
+            z_copy(t, d).wait_send()
+        for d in every:
+            x_copy(t, d).wait_send()
+            s_copy(t, 0, d).wait_send()
+            s_copy(t, 1, d).wait_send()
+
+
+def forward(tokens, out_grad, w_gate, w_up, w_down, weight, shards, chunks):
+    tok_rows, features = tokens.shape
+    rows = shards * tok_rows
     experts, depth, width = w_gate.shape
-    group = min(2, experts)
-    weight_spec = pl.BlockSpec((group, features, width), lambda c, b: (b, c, 0))
-    whole = pl.BlockSpec((experts, rows, width), lambda c, b: (0, 0, 0))
-    out = jax.ShapeDtypeStruct((experts, rows, width), F32)
+    any_spec = pl.BlockSpec(memory_space=pl.ANY)
+    vmem_spec = pl.BlockSpec(memory_space=pltpu.VMEM)
+    gathered = jax.ShapeDtypeStruct((chunks, rows, features), BF16)
+    total = pltpu.VMEM((experts, rows, width), F32)
+    dma = pltpu.SemaphoreType.DMA
     return pl.pallas_call(
-        pre_kernel,
-        grid=(chunks, experts // group),
-        in_specs=[
-            pl.BlockSpec((1, rows, features), lambda c, b: (c, 0, 0)),
-            weight_spec,
-            weight_spec,
-        ],
-        out_specs=[whole, whole],
-        out_shape=[out, out],
-        compiler_params=params(2),
-        cost_estimate=cost(
-            4 * rows * depth * width * experts,
-            2 * rows * depth + 4 * experts * depth * width + 8 * experts * rows * width,
-        ),
-        name="pre_products",
-    )(x_all, w_gate, w_up)
-
-
-def back_kernel(
-    g_ref, down_ref, pre_gate_ref, pre_up_ref, weight_ref,
-    grads_ref, scaled_act_ref, scores_ref, back_ref,
-):
-    c, block = pl.program_id(0), pl.program_id(1)
-    last = pl.num_programs(0) - 1
-    group, width = down_ref.shape[0], down_ref.shape[1]
-    experts = back_ref.shape[0]
-    for i in range(group):
-        e = block * group + i
-        new = dot_nt(g_ref[0], down_ref[i])
-
-        @pl.when(c == 0)
-        def _():
-            back_ref[e] = new
-
-        @pl.when(c > 0)
-        def _():
-            back_ref[e] += new
-
-    @pl.when((c == last) & (block == pl.num_programs(1) - 1))
-    def _():
-        for e in range(experts):
-            pre_gate = pre_gate_ref[e]
-            pre_up = pre_up_ref[e]
-            back = back_ref[e]
-            r = weight_ref[:, e : e + 1]
-            sig = jax.nn.sigmoid(pre_gate)
-            silu = pre_gate * sig
-            act = silu * pre_up
-            scores_ref[:, e : e + 1] = jnp.sum(act * back, axis=1, keepdims=True)
-            scaled = r * back
-            grads_ref[:, e * width : (e + 1) * width] = (
-                scaled * pre_up * sig * (1.0 + pre_gate * (1.0 - sig))
-            ).astype(BF16)
-            at = (experts + e) * width
-            grads_ref[:, at : at + width] = (scaled * silu).astype(BF16)
-            scaled_act_ref[e * width : (e + 1) * width, :] = (r * act).T.astype(BF16)
-
-
-def back_products(g_all, w_down, pre_gate, pre_up, weight):
-    chunks, rows, features = g_all.shape
-    experts, width, depth = w_down.shape
-    group = min(2, experts)
-    whole = pl.BlockSpec((experts, rows, width), lambda c, b: (0, 0, 0))
-    return pl.pallas_call(
-        back_kernel,
-        grid=(chunks, experts // group),
-        in_specs=[
-            pl.BlockSpec((1, rows, features), lambda c, b: (c, 0, 0)),
-            pl.BlockSpec((group, width, features), lambda c, b: (b, 0, c)),
-            whole,
-            whole,
-            pl.BlockSpec((rows, experts), lambda c, b: (0, 0)),
-        ],
-        out_specs=[
-            pl.BlockSpec((rows, 2 * experts * width), lambda c, b: (0, 0)),
-            pl.BlockSpec((experts * width, rows), lambda c, b: (0, 0)),
-            pl.BlockSpec((rows, experts), lambda c, b: (0, 0)),
-        ],
+        forward_kernel,
+        in_specs=[any_spec] * 5 + [vmem_spec],
+        out_specs=[any_spec] * 2 + [vmem_spec] * 3,
         out_shape=[
+            gathered,
+            gathered,
             jax.ShapeDtypeStruct((rows, 2 * experts * width), BF16),
             jax.ShapeDtypeStruct((experts * width, rows), BF16),
             jax.ShapeDtypeStruct((rows, experts), F32),
         ],
-        scratch_shapes=[pltpu.VMEM((experts, rows, width), F32)],
-        compiler_params=params(2),
+        scratch_shapes=[
+            total,
+            total,
+            total,
+            dma((2, shards)),
+            dma((2, shards)),
+            dma((2, shards)),
+            dma((2, shards)),
+            dma((2, 2 * shards)),
+            dma((2, 2 * shards)),
+            dma((2,)),
+        ],
+        compiler_params=pltpu.CompilerParams(
+            vmem_limit_bytes=VMEM_BYTES, collective_id=0, has_side_effects=True
+        ),
         cost_estimate=cost(
-            2 * rows * depth * width * experts,
-            2 * rows * depth + 2 * experts * depth * width + 8 * experts * rows * width,
+            6 * rows * depth * width * experts,
+            8 * rows * depth + 6 * experts * depth * width,
         ),
-        name="back_products",
-    )(g_all, w_down, pre_gate, pre_up, weight)
+        name="forward",
+    )(tokens, out_grad, w_gate, w_up, w_down, weight)
 
 
 def row_kernel(grads_ref, gate_ref, up_ref, out_ref):
@@ -242,22 +344,21 @@
     local_experts, depth, width = w_gate.shape
     first_expert = lax.axis_index("expert") * local_experts
 
-    x_all = lax.all_gather(tokens, BOTH, axis=0, tiled=False).reshape(
-        feature_shards, rows, features
-    )
-    g_all = lax.all_gather(out_grad, BOTH, axis=0, tiled=False).reshape(
-        feature_shards, rows, features
-    )
     local_ids = first_expert + jnp.arange(local_experts, dtype=jnp.int32)
     hit = routes[:, :, None] == local_ids[None, None, :]
     weight = jnp.sum(jnp.where(hit, route_weights[:, :, None], 0.0), axis=1)
 
-    if features % 256 == 0:
-        pre_gate, pre_up = pre_products(x_all, w_gate, w_up)
-        grads, act_t, scores = back_products(g_all, w_down, pre_gate, pre_up, weight)
+    if feature_shards == 4 and features % 256 == 0:
+        x_all, g_all, grads, act_t, scores = forward(
+            tokens, out_grad, w_gate, w_up, w_down, weight, shards, feature_shards
+        )
         part = row_products(grads, w_gate, w_up, feature_shards, 2, 0, features)
         weight_grads = lambda: weight_products(x_all, g_all, grads, act_t, local_experts, 2)
     else:
+        x_all = lax.all_gather(tokens, BOTH, axis=0, tiled=False)
+        g_all = lax.all_gather(out_grad, BOTH, axis=0, tiled=False)
+        x_all = x_all.reshape(feature_shards, rows, features)
+        g_all = g_all.reshape(feature_shards, rows, features)
         part, scores, weight_grads = plain(x_all, g_all, weight, w_gate, w_up, w_down)
 
     part = part.reshape(feature_shards * shards, tok_rows, features)

time: 298 us -> 261 us (0.88)
  waiting for transfers between devices: 168 us -> 59.4 us
  Pallas kernels: 105 us -> 174 us
    all_gather x2 -> x0, waiting for transfers between devices: 114 us -> none  [the longest x1 69.5 us: body(): lax.all_gather(tokens, BOTH, axis=0, tiled=False)]
    pallas_call x2 -> x1, Pallas kernels: 50.5 us -> 120 us  [forward(): pl.pallas_call(forward_kernel, in_specs=[any_spec] * 5 + [vmem_spec], out...]
    reduce_scatter x1, waiting for transfers between devices: 53 us -> 59.3 us  [body(): lax.psum_scatter(part, BOTH, scatter_dimension=0, tiled=True)[0]]
  transfers between devices with their start and end apart: 4 -> 2, of which waited for: 3 -> 1; matrix products, arithmetic and copies ran while one was open for 1% -> 0% of each run, Pallas kernels for 27% -> 21%
where the time goes in v2:
time: 261 us; the launch traced here: 259 us
  Pallas kernels  174 us (67%)
  waiting for transfers between devices  59.4 us (23%)
  between operations  14.1 us (5%)
  blocking collectives  7.57 us (3%)
    pallas_call x1, Pallas kernels, forward(): pl.pallas_call(forward_kernel, in_specs=[any_spec] * 5 + [vmem_spec], out...  120 us
    reduce_scatter x1, waiting for transfers between devices, body(): lax.psum_scatter(part, BOTH, scatter_dimension=0, tiled=True)[0]  59.3 us
    pallas_call x1, Pallas kernels, weight_products(): pl.pallas_call(weight_kernel, grid=(chunks, steps), in_specs=[token_spec,...  30.8 us
    pallas_call x1, Pallas kernels, row_products(): pl.pallas_call(row_kernel, grid=(chunks, steps), in_specs=[pl.BlockSpec(g...  22.9 us
    psum x1, blocking collectives, body(): lax.psum(lax.psum_scatter(picked, 'seq', scatter_dimension=0, tiled=True)...  7.57 us
  transfers between devices with their start and end apart: 2, of which 1 were waited for; matrix products, arithmetic and copies ran while one was open for 0% of the time, Pallas kernels for 21%

profile of v2, /device:TPU:13, one launch (start us, length us, event | category | flops | bytes accessed | tf_op | source)
XLA Modules:
  0.0 258.6 jit_solution(10648786647115313321)
XLA Ops:
  7.2 0.0 reduce-scatter.5.cloned.1.call-start
  7.2 0.8 fusion
  8.1 0.9 copy.14.weight_ref
  8.9 0.0 copy-start
  8.9 120.2 %forward.1 = (bf16[4,512,1792]{2,1,0:T(8,128)(2,1)}, bf16[4,512,1792]{2,1,0:T(8,128)(2,1)}, bf16[512,2048]{1,0:T(8,128)(2,1)}, bf16[1024,512]{1,0:T(8,128)(2,1)}, f32[512,4]{1,0:T(8,128)}) custom-call(bf16[128,1792]{1,0:T(8,128)(2,1)} %tokens_ref.1, bf16[128,1792]{1,0:T(8,128)(2,1)} %grad_ref.1, bf16[4,7168,256]{2,1,0:T(8,128)(2,1)} %gate_ref.3, ...), custom_call_target="tpu_custom_call" | custom-call | flops 22548578304 | bytes 73400320 | tf_op jit(solution)/shard_map/forward/pallas_call | solution.py:222
  129.2 1.1 copy.15
  130.2 0.0 copy-done
  130.2 0.7 fusion.1
  130.9 0.0 reduce-scatter.5.cloned.1.call-update
  130.9 0.2 reduce-scatter.3.cloned.1.call-start
  131.2 22.9 %row_products.1 = bf16[4,512,1792]{2,1,0:T(8,128)(2,1)} custom-call(bf16[512,2048]{1,0:T(8,128)(2,1)} %get-tuple-element.13.grads_ref, bf16[4,7168,256]{2,1,0:T(8,128)(2,1)} %gate_ref.3, bf16[4,7168,256]{2,1,0:T(8,128)(2,1)} %up_ref.3), custom_call_target="tpu_custom_call" | custom-call | flops 15032385536 | bytes 36700160 | tf_op jit(solution)/shard_map/row_products/pallas_call | solution.py:275
  154.0 0.0 reduce-scatter.3.cloned.1.call-update
  154.1 30.8 %weight_products.1 = (bf16[4,7168,256]{2,1,0:T(8,128)(2,1)}, bf16[4,7168,256]{2,1,0:T(8,128)(2,1)}, bf16[4,256,7168]{2,1,0:T(8,128)(2,1)}) custom-call(bf16[4,512,1792]{2,1,0:T(8,128)(2,1)} %get-tuple-element.14.x_ref, bf16[4,512,1792]{2,1,0:T(8,128)(2,1)} %get-tuple-element.15.g_ref, bf16[512,2048]{1,0:T(8,128)(2,1)} %get-tuple-element.13.grads_ref, ...), custom_call_target="tpu_custom_call" | custom-call | flops 22548578304 | bytes 58720256 | tf_op jit(solution)/shard_map/weight_products/pallas_call | solution.py:311
  184.9 0.0 reduce-scatter.5.cloned.1.call-done
  184.9 7.6 %psum.7 = f32[128,8]{0,1:T(8,128)} all-reduce(f32[128,8]{0,1:T(8,128)} %reduce-scatter.5.cloned.1.call-done), channel_id=1, replica_groups=mesh['groups'=2,'expert'=4,'seq'=4] {'expert'}, use_global_device_ids=true, to_apply=%region_4.5 | all-reduce | flops 1024 | bytes 8192 | tf_op jit(solution)/shard_map/psum | solution.py:367
  192.5 59.3 %reduce-scatter.3.cloned.1.call-done = bf16[1,128,1792]{2,1,0:T(8,128)(2,1)} async-done(((bf16[16,128,1792]{2,1,0:T(8,128)(2,1)}), bf16[1,128,1792]{2,1,0:T(8,128)(2,1)}) %reduce-scatter.3.cloned.1.call-update) | async-done | bytes 458768 | tf_op jit(solution)/shard_map/reduce_scatter | solution.py:365
  (1 shorter events, 0.0 us)
Async XLA Ops:
  7.2 177.7 %reduce-scatter.5.cloned.1.call-start = ((), (), s32[]{:S(2)}) async-start(), calls=%async_computation.3 | async-start | bytes 20480 | tf_op jit(solution)/shard_map/reduce_scatter | solution.py:367
  8.9 121.3 %copy-start = (s32[512,8]{0,1:T(8,128)S(1)}, s32[512,8]{0,1:T(8,128)}, u32[]{:S(2)}) copy-start(s32[512,8]{0,1:T(8,128)} %param.9) | copy-start | bytes 49156
  130.9 120.9 %reduce-scatter.3.cloned.1.call-start = ((), (), s32[]{:S(2)}) async-start(), calls=%async_computation.2 | async-start | bytes 7798784 | tf_op jit(solution)/shard_map/reduce_scatter | solution.py:365
Sparse Core Ops, SparseCore 0:
  131.1 19.9 reduce-scatter.4
  156.1 95.6 reduce-scatter.2

commit v3 on v2

--- a/solution.py
+++ b/solution.py
@@ -253,7 +253,7 @@
     )(tokens, out_grad, w_gate, w_up, w_down, weight)
 
 
-def row_kernel(grads_ref, gate_ref, up_ref, out_ref):
+def row_kernel(ids_ref, grads_ref, gate_ref, up_ref, out_ref):
     experts, _, width = gate_ref.shape
     total = None
     for e in range(experts):
@@ -264,76 +264,96 @@
     out_ref[0] = total.astype(BF16)
 
 
-def row_products(grads, w_gate, w_up, chunks, steps, first, count):
+def row_products(grads, w_gate, w_up, ids, features, steps):
     rows = grads.shape[0]
     experts, depth, width = w_gate.shape
-    features = depth // chunks
-    cut = count // steps
-    weight_spec = pl.BlockSpec(
-        (experts, cut, width), lambda c, n: (0, c * (features // cut) + first // cut + n, 0)
-    )
+    count = ids.shape[0]
+    cut = features // steps
+    weight_spec = pl.BlockSpec((experts, cut, width), lambda c, n, ids: (0, ids[c] * steps + n, 0))
     return pl.pallas_call(
         row_kernel,
+        grid_spec=pltpu.PrefetchScalarGridSpec(
+            num_scalar_prefetch=1,
+            grid=(count, steps),
+            in_specs=[
+                pl.BlockSpec(grads.shape, lambda c, n, ids: (0, 0)),
+                weight_spec,
+                weight_spec,
+            ],
+            out_specs=pl.BlockSpec((1, rows, cut), lambda c, n, ids: (c, 0, n)),
+        ),
+        out_shape=jax.ShapeDtypeStruct((count, rows, features), BF16),
+        compiler_params=params(2),
+        cost_estimate=cost(
+            4 * rows * count * features * width * experts,
+            2 * rows * count * features + 4 * experts * count * features * width,
+        ),
+        name="row_products",
+    )(ids, grads, w_gate, w_up)
+
+
+def tall_kernel(x_ref, grads_ref, out_ref):
+    experts, _, width = out_ref.shape
+    x_t = x_ref[0].T
+    for e in range(experts):
+        out_ref[e] = dot_nn(x_t, grads_ref[:, e * width : (e + 1) * width]).astype(BF16)
+
+
+def wide_kernel(g_ref, act_ref, out_ref):
+    experts, width, _ = out_ref.shape
+    for e in range(experts):
+        out_ref[e] = dot_nn(act_ref[e * width : (e + 1) * width, :], g_ref[0]).astype(BF16)
+
+
+def weight_products(kernel, source, factor, factor_shape, half, out_shape, tall, steps):
+    chunks, rows, features = source.shape
+    cut = features // steps
+    experts = out_shape[0]
+    if tall:
+        out_spec = pl.BlockSpec((experts, cut, out_shape[2]), lambda c, n: (0, c * steps + n, 0))
+    else:
+        out_spec = pl.BlockSpec((experts, out_shape[1], cut), lambda c, n: (0, 0, c * steps + n))
+    size = out_shape[0] * out_shape[1] * out_shape[2]
+    return pl.pallas_call(
+        kernel,
         grid=(chunks, steps),
         in_specs=[
-            pl.BlockSpec(grads.shape, lambda c, n: (0, 0)),
-            weight_spec,
-            weight_spec,
+            pl.BlockSpec((1, rows, cut), lambda c, n: (c, 0, n)),
+            pl.BlockSpec(factor_shape, lambda c, n: (0, half)),
         ],
-        out_specs=pl.BlockSpec((1, rows, cut), lambda c, n: (c, 0, n)),
-        out_shape=jax.ShapeDtypeStruct((chunks, rows, count), BF16),
+        out_specs=out_spec,
+        out_shape=jax.ShapeDtypeStruct(out_shape, BF16),
         compiler_params=params(2),
-        cost_estimate=cost(
-            4 * rows * chunks * count * width * experts,
-            2 * rows * chunks * count + 4 * experts * chunks * count * width,
-        ),
-        name="row_products",
-    )(grads, w_gate, w_up)
-
-
-def weight_kernel(x_ref, g_ref, grads_ref, act_ref, gate_ref, up_ref, down_ref):
-    experts, _, width = gate_ref.shape
-    x_t = x_ref[0].T
-    for e in range(experts):
-        gate_ref[e] = dot_nn(x_t, grads_ref[:, e * width : (e + 1) * width]).astype(BF16)
-        at = (experts + e) * width
-        up_ref[e] = dot_nn(x_t, grads_ref[:, at : at + width]).astype(BF16)
-        down_ref[e] = dot_nn(act_ref[e * width : (e + 1) * width, :], g_ref[0]).astype(BF16)
-
-
-def weight_products(x_all, g_all, grads, act_t, experts, steps):
-    chunks, rows, features = x_all.shape
-    width = act_t.shape[0] // experts
-    depth = chunks * features
-    cut = features // steps
-    token_spec = pl.BlockSpec((1, rows, cut), lambda c, n: (c, 0, n))
-    tall = pl.BlockSpec((experts, cut, width), lambda c, n: (0, c * steps + n, 0))
-    return pl.pallas_call(
-        weight_kernel,
-        grid=(chunks, steps),
-        in_specs=[
-            token_spec,
-            token_spec,
-            pl.BlockSpec(grads.shape, lambda c, n: (0, 0)),
-            pl.BlockSpec(act_t.shape, lambda c, n: (0, 0)),
-        ],
-        out_specs=[
-            tall,
-            tall,
-            pl.BlockSpec((experts, width, cut), lambda c, n: (0, 0, c * steps + n)),
-        ],
-        out_shape=[
-            jax.ShapeDtypeStruct((experts, depth, width), BF16),
-            jax.ShapeDtypeStruct((experts, depth, width), BF16),
-            jax.ShapeDtypeStruct((experts, width, depth), BF16),
-        ],
-        compiler_params=params(2),
-        cost_estimate=cost(
-            6 * rows * depth * width * experts,
-            4 * rows * depth + 6 * experts * depth * width,
-        ),
+        cost_estimate=cost(2 * rows * size, 2 * rows * chunks * features + 2 * size),
         name="weight_products",
-    )(x_all, g_all, grads, act_t)
+    )(source, factor)
+
+
+def scatter_rows(grads, w_gate, w_up, features, shards, tok_rows):
+    me = lax.axis_index("expert")
+    z = lax.axis_index("seq")
+    sib = me + 1 - 2 * (me % 2)
+    partner, far = (me + 2) % 4, (sib + 2) % 4
+    to_sib = [(i, i ^ 1) for i in range(4)]
+    to_partner = [(i, (i + 2) % 4) for i in range(4)]
+    sent = row_products(grads, w_gate, w_up, jnp.stack([far, sib]), features, 2)
+    first = lax.ppermute(sent[0], "expert", to_sib)
+    second = lax.ppermute(sent[1], "expert", to_sib)
+    kept = row_products(grads, w_gate, w_up, jnp.stack([partner, me]), features, 2)
+
+    def cut(array, d):
+        return lax.dynamic_slice_in_dim(array, (z + d) % shards * tok_rows, tok_rows, 0)
+
+    total = None
+    for d in [*range(1, shards), 0]:
+        there = cut(kept[0], d).astype(F32) + cut(first, d).astype(F32)
+        there = lax.ppermute(there.astype(BF16), "expert", to_partner)
+        here = cut(kept[1], d).astype(F32) + cut(second, d).astype(F32) + there.astype(F32)
+        if d:
+            along = [(i, (i + d) % shards) for i in range(shards)]
+            here = lax.ppermute(here.astype(BF16), "seq", along).astype(F32)
+        total = here if total is None else total + here
+    return total.astype(BF16)
 
 
 def body(tokens, out_grad, routes, route_weights, w_gate, w_up, w_down):
@@ -352,17 +372,25 @@
         x_all, g_all, grads, act_t, scores = forward(
             tokens, out_grad, w_gate, w_up, w_down, weight, shards, feature_shards
         )
-        part = row_products(grads, w_gate, w_up, feature_shards, 2, 0, features)
-        weight_grads = lambda: weight_products(x_all, g_all, grads, act_t, local_experts, 2)
+        token_grad = scatter_rows(grads, w_gate, w_up, features, shards, tok_rows)
+        half = (rows, local_experts * width)
+
+        def weight_grads():
+            return (
+                weight_products(tall_kernel, x_all, grads, half, 0, w_gate.shape, True, 2),
+                weight_products(tall_kernel, x_all, grads, half, 1, w_up.shape, True, 2),
+                weight_products(wide_kernel, g_all, act_t, act_t.shape, 0, w_down.shape, False, 2),
+            )
+
     else:
         x_all = lax.all_gather(tokens, BOTH, axis=0, tiled=False)
         g_all = lax.all_gather(out_grad, BOTH, axis=0, tiled=False)
         x_all = x_all.reshape(feature_shards, rows, features)
         g_all = g_all.reshape(feature_shards, rows, features)
         part, scores, weight_grads = plain(x_all, g_all, weight, w_gate, w_up, w_down)
-
-    part = part.reshape(feature_shards * shards, tok_rows, features)
-    token_grad = lax.psum_scatter(part, BOTH, scatter_dimension=0, tiled=True)[0]
+        part = part.reshape(feature_shards * shards, tok_rows, features)
+        token_grad = lax.psum_scatter(part, BOTH, scatter_dimension=0, tiled=True)[0]
+
     picked = jnp.sum(jnp.where(hit, scores[:, None, :], 0.0), axis=2)
     gate_grad = lax.psum(lax.psum_scatter(picked, "seq", scatter_dimension=0, tiled=True), "expert")
     grad_gate, grad_up, grad_down = weight_grads()

time: 261 us -> 276 us (1.057)
  waiting for transfers between devices: 59.4 us -> 30 us
  Pallas kernels: 174 us -> 192 us
  starting transfers between devices: 0.26 us -> 12.1 us
  other arithmetic: 1.52 us -> 9.79 us
  local copies, waits for them, and re-layouts: 1.92 us -> 8.68 us
    reduce_scatter x1 -> x0, waiting for transfers between devices: 59.3 us -> none  [body(): lax.psum_scatter(part, BOTH, scatter_dimension=0, tiled=True)[0]]
    ppermute x0 -> x9, waiting for transfers between devices: none -> 30 us  [the longest x3 16 us: scatter_rows(): here = lax.ppermute(here.astype(BF16), 'seq', along).astype(F32)]
    pallas_call x2 -> x5, Pallas kernels: 53.7 us -> 71.6 us  [the longest x3 43.5 us: weight_products(): pl.pallas_call(kernel, grid=(chunks, steps), in_specs=[pl.BlockSpec((1, r...]
    ppermute x0 -> x9, starting transfers between devices: none -> 12.1 us  [the longest x3 7.11 us: scatter_rows(): here = lax.ppermute(here.astype(BF16), 'seq', along).astype(F32)]
    convert_element_type x0 -> x3, other arithmetic: none -> 7.09 us  [the longest x1 2.68 us: scatter_rows(): return total.astype(BF16)]
    squeeze x0 -> x1, local copies, waits for them, and re-layouts: none -> 4.16 us  [scatter_rows(): second = lax.ppermute(sent[1], 'expert', to_sib)]
    slice x0 -> x1, local copies, waits for them, and re-layouts: none -> 3.54 us  [scatter_rows(): kept[1]]
  transfers between devices with their start and end apart: 2 -> 10, of which waited for: 1 -> 4; matrix products, arithmetic and copies ran while one was open for 0% -> 3% of each run, Pallas kernels for 21% -> 21%
where the time goes in v3:
time: 276 us; the launch traced here: 275 us
  Pallas kernels  192 us (70%)
  waiting for transfers between devices  30 us (11%)
  between operations  14.1 us (5%)
  starting transfers between devices  12.1 us (4%)
  other arithmetic  9.79 us (4%)
  local copies, waits for them, and re-layouts  8.68 us (3%)
  blocking collectives  8.53 us (3%)
    pallas_call x1, Pallas kernels, forward(): pl.pallas_call(forward_kernel, in_specs=[any_spec] * 5 + [vmem_spec], out...  120 us
    pallas_call x3, Pallas kernels, weight_products(): pl.pallas_call(kernel, grid=(chunks, steps), in_specs=[pl.BlockSpec((1, r...  43.5 us
    pallas_call x2, Pallas kernels, row_products(): pl.pallas_call(row_kernel, grid_spec=pltpu.PrefetchScalarGridSpec(num_sca...  28.1 us
    ppermute x3, waiting for transfers between devices, scatter_rows(): here = lax.ppermute(here.astype(BF16), 'seq', along).astype(F32)  16 us
    ppermute x4, waiting for transfers between devices, scatter_rows(): there = lax.ppermute(there.astype(BF16), 'expert', to_partner)  14 us
    psum x1, blocking collectives, body(): lax.psum(lax.psum_scatter(picked, 'seq', scatter_dimension=0, tiled=True)...  8.53 us
    ppermute x3, starting transfers between devices, scatter_rows(): here = lax.ppermute(here.astype(BF16), 'seq', along).astype(F32)  7.11 us
  transfers between devices with their start and end apart: 10, of which 4 were waited for; matrix products, arithmetic and copies ran while one was open for 3% of the time, Pallas kernels for 21%

profile of v3, /device:TPU:13, one launch (start us, length us, event | category | flops | bytes accessed | tf_op | source)
XLA Modules:
  0.0 275.1 jit_solution(8613169576160867080)
XLA Ops:
  7.2 0.0 reduce-scatter.2.cloned.1.call-start
  7.3 0.8 fusion.13
  8.1 0.9 copy.14.weight_ref
  8.9 0.6 pad_add_fusion.1.ids_ref
  9.5 120.2 %forward.1 = (bf16[4,512,1792]{2,1,0:T(8,128)(2,1)}, bf16[4,512,1792]{2,1,0:T(8,128)(2,1)}, bf16[512,2048]{1,0:T(8,128)(2,1)}, bf16[1024,512]{1,0:T(8,128)(2,1)}, f32[512,4]{1,0:T(8,128)}) custom-call(bf16[128,1792]{1,0:T(8,128)(2,1)} %tokens_ref.1, bf16[128,1792]{1,0:T(8,128)(2,1)} %grad_ref.1, bf16[4,7168,256]{2,1,0:T(8,128)(2,1)} %gate_ref.5, ...), custom_call_target="tpu_custom_call" | custom-call | flops 22548578304 | bytes 73400320 | tf_op jit(solution)/shard_map/forward/pallas_call | solution.py:222
  129.7 13.9 %row_products.3 = bf16[2,512,1792]{2,1,0:T(8,128)(2,1)} custom-call(s32[2]{0:T(128)} %pad_add_fusion.1.ids_ref, bf16[512,2048]{1,0:T(8,128)(2,1)} %get-tuple-element.10.grads_ref, bf16[4,7168,256]{2,1,0:T(8,128)(2,1)} %gate_ref.5, bf16[4,7168,256]{2,1,0:T(8,128)(2,1)} %up_ref.5), custom_call_target="tpu_custom_call" | custom-call | flops 7516192768 | bytes 18350080 | tf_op jit(solution)/shard_map/row_products/pallas_call | solution.py:273
  143.7 4.2 %slice_bitcast_fusion.1 = (bf16[512,1792]{1,0:T(8,128)(2,1)}, bf16[512,1792]{1,0:T(8,128)(2,1)}) fusion(bf16[2,512,1792]{2,1,0:T(8,128)(2,1)} %row_products.3), kind=kLoop, calls=%fused_computation.1 | loop fusion | bytes 7340032 | tf_op jit(solution)/shard_map/squeeze | solution.py:341
  147.8 2.0 collective-permute-start.1
  149.8 0.1 copy.15
  149.9 0.7 fusion.14
  150.6 0.0 reduce-scatter.2.cloned.1.call-update
  150.7 0.6 pad_add_fusion.ids_ref
  151.3 14.1 %row_products.2 = bf16[2,512,1792]{2,1,0:T(8,128)(2,1)} custom-call(s32[2]{0:T(128)} %pad_add_fusion.ids_ref, bf16[512,2048]{1,0:T(8,128)(2,1)} %get-tuple-element.10.grads_ref, bf16[4,7168,256]{2,1,0:T(8,128)(2,1)} %gate_ref.5, bf16[4,7168,256]{2,1,0:T(8,128)(2,1)} %up_ref.5), custom_call_target="tpu_custom_call" | custom-call | flops 7516192768 | bytes 18350080 | tf_op jit(solution)/shard_map/row_products/pallas_call | solution.py:273
  165.4 3.5 %fusion.15 = (bf16[1,512,1792]{2,1,0:T(8,128)(2,1)S(1)}, bf16[1,512,1792]{2,1,0:T(8,128)(2,1)}) fusion(bf16[2,512,1792]{2,1,0:T(8,128)(2,1)} %row_products.2), kind=kLoop, calls=%fused_computation.30 | loop fusion | bytes 7340032 | tf_op jit(solution)/shard_map/slice | solution.py:351
  168.9 14.4 %weight_products.3 = bf16[4,7168,256]{2,1,0:T(8,128)(2,1)} custom-call(bf16[4,512,1792]{2,1,0:T(8,128)(2,1)} %get-tuple-element.11.x_ref, bf16[512,2048]{1,0:T(8,128)(2,1)} %get-tuple-element.10.grads_ref), custom_call_target="tpu_custom_call" | custom-call | flops 7516192768 | bytes 22020096 | tf_op jit(solution)/shard_map/weight_products/pallas_call | solution.py:317
  183.3 1.9 fusion.10
  185.2 0.1 collective-permute-start.2
  185.3 1.5 collective-permute-start.4
  186.7 0.1 collective-permute-start.6
  186.8 14.3 %weight_products.4 = bf16[4,7168,256]{2,1,0:T(8,128)(2,1)} custom-call(bf16[4,512,1792]{2,1,0:T(8,128)(2,1)} %get-tuple-element.11.x_ref, bf16[512,2048]{1,0:T(8,128)(2,1)} %get-tuple-element.10.grads_ref), custom_call_target="tpu_custom_call" | custom-call | flops 7516192768 | bytes 22020096 | tf_op jit(solution)/shard_map/weight_products/pallas_call | solution.py:317
  201.1 1.4 collective-permute-start.8
  202.5 4.2 %collective-permute-done.4 = bf16[128,1792]{1,0:T(8,128)(2,1)S(1)} collective-permute-done((bf16[128,1792]{1,0:T(8,128)(2,1)S(1)}, bf16[128,1792]{1,0:T(8,128)(2,1)S(1)}, u32[]{:S(2)}, u32[]{:S(2)}) %collective-permute-start.4) | collective-permute-done | bytes 458784 | tf_op jit(solution)/shard_map/ppermute | solution.py:350
  206.7 9.8 %collective-permute-done.6 = bf16[128,1792]{1,0:T(8,128)(2,1)S(1)} collective-permute-done((bf16[128,1792]{1,0:T(8,128)(2,1)S(1)}, bf16[128,1792]{1,0:T(8,128)(2,1)S(1)}, u32[]{:S(2)}, u32[]{:S(2)}) %collective-permute-start.6) | collective-permute-done | bytes 458784 | tf_op jit(solution)/shard_map/ppermute | solution.py:350
  216.5 2.6 fusion.12
  219.0 0.7 collective-permute-start.3
  219.8 4.9 %collective-permute-start.5 = (bf16[128,1792]{1,0:T(8,128)(2,1)S(1)}, bf16[128,1792]{1,0:T(8,128)(2,1)}, u32[]{:S(2)}, u32[]{:S(2)}) collective-permute-start(bf16[128,1792]{1,0:T(8,128)(2,1)S(1)} %get-tuple-element.17), channel_id=1, source_target_pairs={{0,2},{1,3},{2,0},{3,1},{4,6},{5,7},{6,4},{7,5},{8,10},{9,11},{10,... | collective-permute-start | bytes 1376264 | tf_op jit(solution)/shard_map/ppermute | solution.py:354
  224.7 1.5 collective-permute-start.7
  226.2 14.8 %weight_products.5 = bf16[4,256,7168]{2,1,0:T(8,128)(2,1)} custom-call(bf16[4,512,1792]{2,1,0:T(8,128)(2,1)} %get-tuple-element.12.g_ref, bf16[1024,512]{1,0:T(8,128)(2,1)} %get-tuple-element.13.act_ref), custom_call_target="tpu_custom_call" | custom-call | flops 7516192768 | bytes 22020096 | tf_op jit(solution)/shard_map/weight_products/pallas_call | solution.py:317
  241.0 8.5 %psum.7 = f32[128,8]{0,1:T(8,128)} all-reduce(f32[128,8]{0,1:T(8,128)} %reduce-scatter.2.cloned.1.call-done), channel_id=1, replica_groups=mesh['groups'=2,'expert'=4,'seq'=4] {'expert'}, use_global_device_ids=true, to_apply=%region_3.4 | all-reduce | flops 1024 | bytes 8192 | tf_op jit(solution)/shard_map/psum | solution.py:395
  249.6 7.5 %collective-permute-done.5 = bf16[128,1792]{1,0:T(8,128)(2,1)} collective-permute-done((bf16[128,1792]{1,0:T(8,128)(2,1)S(1)}, bf16[128,1792]{1,0:T(8,128)(2,1)}, u32[]{:S(2)}, u32[]{:S(2)}) %collective-permute-start.5) | collective-permute-done | bytes 458784 | tf_op jit(solution)/shard_map/ppermute | solution.py:354
  257.0 8.5 %collective-permute-done.7 = bf16[128,1792]{1,0:T(8,128)(2,1)} collective-permute-done((bf16[128,1792]{1,0:T(8,128)(2,1)S(1)}, bf16[128,1792]{1,0:T(8,128)(2,1)}, u32[]{:S(2)}, u32[]{:S(2)}) %collective-permute-start.7) | collective-permute-done | bytes 458784 | tf_op jit(solution)/shard_map/ppermute | solution.py:354
  265.5 2.7 fusion.3
  (14 shorter events, 0.0 us)
Async XLA Ops:
  7.2 233.9 %reduce-scatter.2.cloned.1.call-start = ((), (), s32[]{:S(2)}) async-start(), calls=%async_computation.1 | async-start | bytes 20480 | tf_op jit(solution)/shard_map/reduce_scatter | solution.py:395
  143.7 6.2 %copy-start.1 = (f32[512,4]{1,0:T(8,128)S(1)}, f32[512,4]{1,0:T(8,128)}, u32[]{:S(2)}) copy-start(f32[512,4]{1,0:T(8,128)} %get-tuple-element.14) | copy-start | bytes 24580
  143.7 6.3 %copy-start.2 = (s32[512,8]{0,1:T(8,128)S(1)}, s32[512,8]{0,1:T(8,128)}, u32[]{:S(2)}) copy-start(s32[512,8]{0,1:T(8,128)} %param.9) | copy-start | bytes 49156
  147.8 35.5 %collective-permute-start.1 = (bf16[512,1792]{1,0:T(8,128)(2,1)}, bf16[512,1792]{1,0:T(8,128)(2,1)}, u32[]{:S(2)}, u32[]{:S(2)}) collective-permute-start(bf16[512,1792]{1,0:T(8,128)(2,1)} %get-tuple-element.25), channel_id=1, source_target_pairs={{0,4},{4,0},{8,12},{12,8},{1,5},{5,1},{9,13},{13,9},{2,6},{6,2},{1... | collective-permute-start | bytes 5505032 | tf_op jit(solution)/shard_map/ppermute | solution.py:340
  149.8 52.6 %collective-permute-start = (bf16[512,1792]{1,0:T(8,128)(2,1)}, bf16[512,1792]{1,0:T(8,128)(2,1)}, u32[]{:S(2)}, u32[]{:S(2)}) collective-permute-start(bf16[512,1792]{1,0:T(8,128)(2,1)} %get-tuple-element.24), channel_id=1, source_target_pairs={{0,4},{4,0},{8,12},{12,8},{1,5},{5,1},{9,13},{13,9},{2,6},{6,2},{1... | collective-permute-start | bytes 5505032 | tf_op jit(solution)/shard_map/ppermute | solution.py:341
  168.9 14.4 %copy-start = (bf16[1,512,1792]{2,1,0:T(8,128)(2,1)S(1)}, bf16[1,512,1792]{2,1,0:T(8,128)(2,1)}, u32[]{:S(2)}) copy-start(bf16[1,512,1792]{2,1,0:T(8,128)(2,1)} %get-tuple-element.23) | copy-start | bytes 5505028
  185.2 17.3 %collective-permute-start.2 = (bf16[128,1792]{1,0:T(8,128)(2,1)S(1)}, bf16[128,1792]{1,0:T(8,128)(2,1)S(1)}, u32[]{:S(2)}, u32[]{:S(2)}) collective-permute-start(bf16[128,1792]{1,0:T(8,128)(2,1)S(1)} %get-tuple-element.18), channel_id=1, source_target_pairs={{0,8},{4,12},{8,0},{12,4},{1,9},{5,13},{9,1},{13,5},{2,10},{6,14},... | collective-permute-start | bytes 1376264 | tf_op jit(solution)/shard_map/ppermute | solution.py:350
  185.3 21.4 %collective-permute-start.4 = (bf16[128,1792]{1,0:T(8,128)(2,1)S(1)}, bf16[128,1792]{1,0:T(8,128)(2,1)S(1)}, u32[]{:S(2)}, u32[]{:S(2)}) collective-permute-start(bf16[128,1792]{1,0:T(8,128)(2,1)S(1)} %get-tuple-element.21), channel_id=1, source_target_pairs={{0,8},{4,12},{8,0},{12,4},{1,9},{5,13},{9,1},{13,5},{2,10},{6,14},... | collective-permute-start | bytes 1376264 | tf_op jit(solution)/shard_map/ppermute | solution.py:350
  186.7 29.8 %collective-permute-start.6 = (bf16[128,1792]{1,0:T(8,128)(2,1)S(1)}, bf16[128,1792]{1,0:T(8,128)(2,1)S(1)}, u32[]{:S(2)}, u32[]{:S(2)}) collective-permute-start(bf16[128,1792]{1,0:T(8,128)(2,1)S(1)} %get-tuple-element.20), channel_id=1, source_target_pairs={{0,8},{4,12},{8,0},{12,4},{1,9},{5,13},{9,1},{13,5},{2,10},{6,14},... | collective-permute-start | bytes 1376264 | tf_op jit(solution)/shard_map/ppermute | solution.py:350
  201.1 48.5 %collective-permute-start.8 = (bf16[128,1792]{1,0:T(8,128)(2,1)S(1)}, bf16[128,1792]{1,0:T(8,128)(2,1)}, u32[]{:S(2)}, u32[]{:S(2)}) collective-permute-start(bf16[128,1792]{1,0:T(8,128)(2,1)S(1)} %get-tuple-element.19), channel_id=1, source_target_pairs={{0,8},{4,12},{8,0},{12,4},{1,9},{5,13},{9,1},{13,5},{2,10},{6,14},... | collective-permute-start | bytes 1376264 | tf_op jit(solution)/shard_map/ppermute | solution.py:350
  219.0 30.5 %collective-permute-start.3 = (bf16[128,1792]{1,0:T(8,128)(2,1)}, bf16[128,1792]{1,0:T(8,128)(2,1)}, u32[]{:S(2)}, u32[]{:S(2)}) collective-permute-start(bf16[128,1792]{1,0:T(8,128)(2,1)} %get-tuple-element.15), channel_id=1, source_target_pairs={{0,1},{1,2},{2,3},{3,0},{4,5},{5,6},{6,7},{7,4},{8,9},{9,10},{10,1... | collective-permute-start | bytes 1376264 | tf_op jit(solution)/shard_map/ppermute | solution.py:354
  219.8 37.2 %collective-permute-start.5 = (bf16[128,1792]{1,0:T(8,128)(2,1)S(1)}, bf16[128,1792]{1,0:T(8,128)(2,1)}, u32[]{:S(2)}, u32[]{:S(2)}) collective-permute-start(bf16[128,1792]{1,0:T(8,128)(2,1)S(1)} %get-tuple-element.17), channel_id=1, source_target_pairs={{0,2},{1,3},{2,0},{3,1},{4,6},{5,7},{6,4},{7,5},{8,10},{9,11},{10,... | collective-permute-start | bytes 1376264 | tf_op jit(solution)/shard_map/ppermute | solution.py:354
  224.7 40.8 %collective-permute-start.7 = (bf16[128,1792]{1,0:T(8,128)(2,1)S(1)}, bf16[128,1792]{1,0:T(8,128)(2,1)}, u32[]{:S(2)}, u32[]{:S(2)}) collective-permute-start(bf16[128,1792]{1,0:T(8,128)(2,1)S(1)} %get-tuple-element.16), channel_id=1, source_target_pairs={{0,3},{1,0},{2,1},{3,2},{4,7},{5,4},{6,5},{7,6},{8,11},{9,8},{10,9... | collective-permute-start | bytes 1376264 | tf_op jit(solution)/shard_map/ppermute | solution.py:354
Sparse Core Ops, SparseCore 0:
  150.8 18.3 reduce-scatter.1
